TPU v7x, 128 devices: a whole 4x4x4 slice. The times are simulated.
128 devices in a mesh: seq: 32 (over x, z, core), chan: 4 (over y).
Axes of the slice: x: 4, y: 4, z: 4, core: 2. Of those that a mesh axis runs over, the one named last changes fastest.
Arguments:
- signal: bfloat16 [16384, 3072], P('seq', 'chan'), may hold values from -6 to 6
- rates: float32 [32, 3072], P(None, 'chan'), may hold values from 0 to 1, as said below
- freqs: float32 [32, 3072], P(None, 'chan'), may hold values from -1 to 1
- coeffs: float32 [2, 32, 3072], P(None, None, 'chan'), may hold values from -1 to 1
- skip: float32 [3072], P('chan'), may hold values from -4 to 4
- weight: bfloat16 [3072, 3072], P('seq', 'chan'), may hold values from -0.109375 to 0.109375
Outputs:
- mixed: bfloat16 [16384, 3072], P('seq', 'chan')
Inputs may be any that keep to these rules, and one draw needn't show every extreme that they name: Positive decay rates per position.
All inputs are finite; a program needn't handle non-finite values.
Results may differ from a plain program's by a relative error of at most 0.011.
Values may be sent and summed in bfloat16 or wider, within the bound.
No kernel may reach another device: no remote copies, remote signals or barrier semaphores. Data moves between devices by JAX's collectives and lax.ppermute only.
A program may use at most 128 MiB of HBM per device.

v0:
```python
import jax
import jax.numpy as jnp
from jax import lax
from jax.sharding import PartitionSpec as P

BLOCK = 128
SLAB = 128


highest = lax.Precision.HIGHEST
three_pass = lax.Precision.HIGH


def entering(part, axis, combine, identity):
    place = lax.axis_index(axis)
    gathered = jax.tree.map(lambda a: lax.all_gather(a, axis), part)
    state = jax.tree.map(lambda a, e: jnp.zeros_like(a) + jnp.asarray(e, a.dtype), part, identity)

    def one(lap, state):
        return combine(
            state, jax.tree.map(lambda a: lax.dynamic_index_in_dim(a, lap, 0, False), gathered)
        )

    return lax.fori_loop(0, place, one, state)


def mode_powers(decays, angles, count):
    exponents = jnp.arange(count, dtype=jnp.float32)[:, None, None]
    magnitude = jnp.exp(-decays[None] * exponents)
    turned = angles[None] * exponents
    return (magnitude * jnp.cos(turned), magnitude * jnp.sin(turned))


def transform_tables(length):
    period = 2 * length
    bins = length + 1
    freq_ids = jnp.arange(bins, dtype=jnp.int32)[:, None]
    time_ids = jnp.arange(length, dtype=jnp.int32)[None, :]
    phases = 2.0 * jnp.pi / period * (freq_ids * time_ids % period).astype(jnp.float32)
    forward = jnp.concatenate([jnp.cos(phases), -jnp.sin(phases)], axis=0)
    edge = jnp.logical_or(freq_ids == 0, freq_ids == length)
    weights = jnp.where(edge, 1.0, 2.0).astype(jnp.float32)
    inverse = (
        jnp.concatenate([(weights * jnp.cos(phases)).T, -(weights * jnp.sin(phases)).T], axis=1)
        / period
    )
    return (forward, inverse)


def split_product(form, table, data):
    upper = table.astype(jnp.bfloat16)
    lower = (table - upper.astype(jnp.float32)).astype(jnp.bfloat16)
    first = jnp.einsum(form, upper, data, preferred_element_type=jnp.float32)
    return first + jnp.einsum(form, lower, data, preferred_element_type=jnp.float32)


def by_slab(array):
    leading = array.shape[:-1]
    split = array.reshape(leading + (array.shape[-1] // SLAB, SLAB))
    return jnp.moveaxis(split, -2, 0)


def local_slab(operands):
    slab_in, slab_decay, slab_angle, coef_re, coef_im = operands
    tok_rows, width = slab_in.shape
    blocks = tok_rows // BLOCK
    bins = BLOCK + 1
    pow_re, pow_im = mode_powers(slab_decay, slab_angle, BLOCK + 1)
    kernel = 2.0 * jnp.sum(coef_re[None] * pow_re[:BLOCK] - coef_im[None] * pow_im[:BLOCK], axis=1)
    forward, inverse = transform_tables(BLOCK)
    spectrum = jnp.dot(forward, kernel, precision=highest)
    kern_re = spectrum[:bins]
    kern_im = spectrum[bins:]
    values = slab_in.reshape(blocks, BLOCK, width)
    transformed = split_product("ft,bts->bfs", forward, values)
    in_re = transformed[:, :bins]
    in_im = transformed[:, bins:]
    product = jnp.concatenate(
        [in_re * kern_re - in_im * kern_im, in_re * kern_im + in_im * kern_re], axis=1
    )
    inner_out = jnp.einsum("tf,bfs->bts", inverse, product, precision=three_pass)
    back_re = pow_re[BLOCK - 1 :: -1]
    back_im = pow_im[BLOCK - 1 :: -1]
    sums_re = split_product("tns,bts->bns", back_re, values)
    sums_im = split_product("tns,bts->bns", back_im, values)
    step_re = pow_re[BLOCK]
    step_im = pow_im[BLOCK]

    def advance(carry, block_sums):
        hold_re, hold_im, power_re, power_im = carry
        add_re, add_im = block_sums
        next_re = step_re * hold_re - step_im * hold_im + add_re
        next_im = step_re * hold_im + step_im * hold_re + add_im
        grown_re = step_re * power_re - step_im * power_im
        grown_im = step_re * power_im + step_im * power_re
        return ((next_re, next_im, grown_re, grown_im), (hold_re, hold_im, power_re, power_im))

    zero_state = jnp.zeros_like(slab_decay)
    unit_state = jnp.ones_like(slab_decay)
    final_state, starts = lax.scan(
        advance, (zero_state, zero_state, unit_state, zero_state), (sums_re, sums_im)
    )
    return (inner_out.reshape(tok_rows, width), starts, final_state)


def finish_slab(operands):
    (
        slab_in,
        slab_decay,
        slab_angle,
        coef_re,
        coef_im,
        inner_out,
        starts,
        carry_re,
        carry_im,
        slab_skip,
    ) = operands
    tok_rows, width = slab_in.shape
    blocks = tok_rows // BLOCK
    hold_re, hold_im, power_re, power_im = starts
    pow_re, pow_im = mode_powers(slab_decay, slab_angle, BLOCK + 1)
    outer_re = coef_re[None] * pow_re[1:] - coef_im[None] * pow_im[1:]
    outer_im = coef_re[None] * pow_im[1:] + coef_im[None] * pow_re[1:]
    full_re = hold_re + power_re * carry_re[None] - power_im * carry_im[None]
    full_im = hold_im + power_re * carry_im[None] + power_im * carry_re[None]
    correction = jnp.einsum("tns,bns->bts", outer_re, full_re, precision=three_pass)
    correction = correction - jnp.einsum("tns,bns->bts", outer_im, full_im, precision=three_pass)
    values = slab_in.astype(jnp.float32).reshape(blocks, BLOCK, width)
    total = (
        inner_out.reshape(blocks, BLOCK, width) + 2.0 * correction + slab_skip[None, None] * values
    )
    return jax.nn.gelu(total).astype(jnp.bfloat16).reshape(tok_rows, width)


def chain_combine(earlier, later):
    early_pr, early_pi, early_sr, early_si = earlier
    late_pr, late_pi, late_sr, late_si = later
    return (
        early_pr * late_pr - early_pi * late_pi,
        early_pr * late_pi + early_pi * late_pr,
        late_pr * early_sr - late_pi * early_si + late_sr,
        late_pr * early_si + late_pi * early_sr + late_si,
    )


def local(signal, rates, freqs, coeffs, skip, weight):
    tok_rows, channels = signal.shape
    slab_signal = by_slab(signal)
    slab_decay = by_slab(rates)
    slab_angle = by_slab(freqs)
    slab_cre = by_slab(coeffs[0])
    slab_cim = by_slab(coeffs[1])
    slab_skip = by_slab(skip)
    inner_all, starts_all, final_all = lax.map(
        local_slab, (slab_signal, slab_decay, slab_angle, slab_cre, slab_cim)
    )
    end_re, end_im, shard_pr, shard_pi = final_all
    zero_state = jnp.zeros_like(end_re)
    unit_state = jnp.ones_like(end_re)
    prefix = entering(
        (shard_pr, shard_pi, end_re, end_im),
        "seq",
        chain_combine,
        (unit_state, zero_state, zero_state, zero_state),
    )
    carry_re = prefix[2]
    carry_im = prefix[3]
    act_slabs = lax.map(
        finish_slab,
        (
            slab_signal,
            slab_decay,
            slab_angle,
            slab_cre,
            slab_cim,
            inner_all,
            starts_all,
            carry_re,
            carry_im,
            slab_skip,
        ),
    )
    act = jnp.moveaxis(act_slabs, 0, 1).reshape(tok_rows, channels)
    gathered = lax.all_gather(act, "chan", axis=1, tiled=True)
    proj = jnp.dot(
        gathered,
        lax.all_gather(weight, "seq", axis=0, tiled=True),
        preferred_element_type=jnp.float32,
    )
    return (signal.astype(jnp.float32) + proj).astype(jnp.bfloat16)


def solution(mesh):
    in_specs = (
        P("seq", "chan"),
        P(None, "chan"),
        P(None, "chan"),
        P(None, None, "chan"),
        P("chan"),
        P("seq", "chan"),
    )
    out_specs = P("seq", "chan")
    return jax.shard_map(local, mesh=mesh, in_specs=in_specs, out_specs=out_specs, check_vma=False)
```

profile of v0, /device:TPU:28, one launch (start us, length us, event | category | flops | bytes accessed | tf_op | source)
XLA Modules:
  0.0 740.5 jit_solution(9152365207831654842)
XLA Ops:
  12.7 236.8 %while.109 = (s32[]{:T(128)}, f32[6,512,128]{2,1,0:T(8,128)}, f32[6,4,32,128]{3,2,1,0:T(8,128)}, f32[6,4,32,128]{3,2,1,0:T(8,128)}, f32[6,4,32,128]{3,2,1,0:T(8,...) while((s32[]{:T(128)}, f32[6,512,128]{2,1,0:T(8,128)}, ...), condition=%wide.region_4.5_spmd, body=%wide.region_0.4_spmd.sunk | while | flops 246702592 | bytes 66984224 | solution.py:155
  12.8 7.6 %cosine_multiply_fusion.7 = (f32[129,32,128]{2,1,0:T(8,128)S(1)}, f32[129,32,128]{2,1,0:T(8,128)S(1)}) fusion(f32[32,128]{1,0:T(8,128)S(1)} %dynamic-slice_bitcast_fusion.10, f32[32,128]{1,0:T(8,128)S(1)} %negate_bitcast_fusion.4), kind=kLoop, calls=%fused_computation.75.clone.1 | loop fusion | flops 2113536 | bytes 4259840 | tf_op jit(solution)/shard_map/while/body/eval_jaxpr/mul | solution.py:31
  20.5 2.6 fusion.159
  52.2 7.6 %cosine_multiply_fusion.7 = (f32[129,32,128]{2,1,0:T(8,128)S(1)}, f32[129,32,128]{2,1,0:T(8,128)S(1)}) fusion(f32[32,128]{1,0:T(8,128)S(1)} %dynamic-slice_bitcast_fusion.10, f32[32,128]{1,0:T(8,128)S(1)} %negate_bitcast_fusion.4), kind=kLoop, calls=%fused_computation.75.clone.1 | loop fusion | flops 2113536 | bytes 4259840 | tf_op jit(solution)/shard_map/while/body/eval_jaxpr/mul | solution.py:31
  59.9 2.6 fusion.159
  91.6 7.6 %cosine_multiply_fusion.7 = (f32[129,32,128]{2,1,0:T(8,128)S(1)}, f32[129,32,128]{2,1,0:T(8,128)S(1)}) fusion(f32[32,128]{1,0:T(8,128)S(1)} %dynamic-slice_bitcast_fusion.10, f32[32,128]{1,0:T(8,128)S(1)} %negate_bitcast_fusion.4), kind=kLoop, calls=%fused_computation.75.clone.1 | loop fusion | flops 2113536 | bytes 4259840 | tf_op jit(solution)/shard_map/while/body/eval_jaxpr/mul | solution.py:31
  99.3 2.6 fusion.159
  131.1 7.6 %cosine_multiply_fusion.7 = (f32[129,32,128]{2,1,0:T(8,128)S(1)}, f32[129,32,128]{2,1,0:T(8,128)S(1)}) fusion(f32[32,128]{1,0:T(8,128)S(1)} %dynamic-slice_bitcast_fusion.10, f32[32,128]{1,0:T(8,128)S(1)} %negate_bitcast_fusion.4), kind=kLoop, calls=%fused_computation.75.clone.1 | loop fusion | flops 2113536 | bytes 4259840 | tf_op jit(solution)/shard_map/while/body/eval_jaxpr/mul | solution.py:31
  138.8 2.6 fusion.159
  170.5 7.6 %cosine_multiply_fusion.7 = (f32[129,32,128]{2,1,0:T(8,128)S(1)}, f32[129,32,128]{2,1,0:T(8,128)S(1)}) fusion(f32[32,128]{1,0:T(8,128)S(1)} %dynamic-slice_bitcast_fusion.10, f32[32,128]{1,0:T(8,128)S(1)} %negate_bitcast_fusion.4), kind=kLoop, calls=%fused_computation.75.clone.1 | loop fusion | flops 2113536 | bytes 4259840 | tf_op jit(solution)/shard_map/while/body/eval_jaxpr/mul | solution.py:31
  178.2 2.6 fusion.159
  209.9 7.6 %cosine_multiply_fusion.7 = (f32[129,32,128]{2,1,0:T(8,128)S(1)}, f32[129,32,128]{2,1,0:T(8,128)S(1)}) fusion(f32[32,128]{1,0:T(8,128)S(1)} %dynamic-slice_bitcast_fusion.10, f32[32,128]{1,0:T(8,128)S(1)} %negate_bitcast_fusion.4), kind=kLoop, calls=%fused_computation.75.clone.1 | loop fusion | flops 2113536 | bytes 4259840 | tf_op jit(solution)/shard_map/while/body/eval_jaxpr/mul | solution.py:31
  252.2 44.0 %all-gather.15.cloned.1.call-done = f32[192,32,128]{2,1,0:T(8,128)} async-done(((f32[6,32,128]{2,1,0:T(8,128)}), f32[192,32,128]{2,1,0:T(8,128)}) %all-gather.15.cloned.1.call-update) | async-done | bytes 3145744 | tf_op jit(solution)/shard_map/all_gather | solution.py:16
  296.2 46.7 %all-gather.17.cloned.1.call-done = f32[192,32,128]{2,1,0:T(8,128)} async-done(((f32[6,32,128]{2,1,0:T(8,128)}), f32[192,32,128]{2,1,0:T(8,128)}) %all-gather.17.cloned.1.call-update) | async-done | bytes 3145744 | tf_op jit(solution)/shard_map/all_gather | solution.py:16
  342.9 46.8 %all-gather.19.cloned.1.call-done = f32[192,32,128]{2,1,0:T(8,128)} async-done(((f32[6,32,128]{2,1,0:T(8,128)}), f32[192,32,128]{2,1,0:T(8,128)}) %all-gather.19.cloned.1.call-update) | async-done | bytes 3145744 | tf_op jit(solution)/shard_map/all_gather | solution.py:16
  389.7 46.6 %all-gather.21.cloned.1.call-done = f32[192,32,128]{2,1,0:T(8,128)} async-done(((f32[6,32,128]{2,1,0:T(8,128)}), f32[192,32,128]{2,1,0:T(8,128)}) %all-gather.21.cloned.1.call-update) | async-done | bytes 3145744 | tf_op jit(solution)/shard_map/all_gather | solution.py:16
  436.3 18.6 %while.110 = (s32[]{:T(128)}, f32[6,32,128]{2,1,0:T(8,128)S(1)}, f32[6,32,128]{2,1,0:T(8,128)S(1)}, s32[]{:T(128)}, f32[32,6,32,128]{3,2,1,0:T(8,128)}, /*index=...) while((s32[]{:T(128)}, f32[6,32,128]{2,1,0:T(8,128)S(1)}, ...), condition=%wide.region_6.7_spmd, body=%wide.region_5.6_spmd.sunk | while | flops 196613 | bytes 786579 | solution.py:24
  454.9 217.6 %while.111 = (s32[]{:T(128)}, bf16[6,512,128]{1,2,0:T(8,128)(2,1)}, f32[6,512,128]{2,1,0:T(8,128)}, f32[6,4,32,128]{3,2,1,0:T(8,128)}, f32[6,4,32,128]{3,2,1,0:T...) while((s32[]{:T(128)}, bf16[6,512,128]{1,2,0:T(8,128)(2,1)}, ...), condition=%wide.region_8.9_spmd, body=%wide.region_7.8_spmd.sunk | while | flops 32583680 | bytes 18155700 | solution.py:169
  464.1 11.7 %fusion.171 = f32[128,4,128]{2,1,0:T(4,128)S(1)} fusion(f32[32,128]{0,1:T(8,128)S(1)} %get-tuple-element.1112, f32[32,128]{0,1:T(8,128)S(1)} %get-tuple-element.1113, f32[129,32,128]{0,1,2:T(8,128)} %multiply_exponential_fusion.3, f32[129,32,128]{0,1,2:T(8,128)} %iota_multiply_fusion.3, f32[1,4,32,128]{2,1,3,0:T(4,128)S(1)} %copy.94, ...), kind=kOutput, calls=%fused_computation.10.clone.1 | convolution fusion | flops 15269888 | bytes 4718592 | tf_op jit(solution)/shard_map/while/body/eval_jaxpr/tns,bns->bts/dot_general | solution.py:128
  478.9 11.8 %fusion.173 = bf16[4,128,128]{1,0,2:T(4,128)(2,1)S(1)} fusion(f32[4,128,128]{1,0,2:T(4,128)S(1)} %copy.93, f32[128,4,128]{2,1,0:T(4,128)S(1)} %fusion.171, f32[32,128]{0,1:T(8,128)S(1)} %get-tuple-element.1112, f32[32,128]{0,1:T(8,128)S(1)} %get-tuple-element.1113, f32[129,32,128]{0,1,2:T(8,128)} %iota_multiply_fusion.3, ...), kind=kOutput, calls=%fused_computation.37.clone.1 | convolution fusion | flops 16187392 | bytes 5374464 | tf_op jit(solution)/shard_map/while/body/eval_jaxpr/tns,bns->bts/dot_general | solution.py:127
  500.5 11.6 %fusion.171 = f32[128,4,128]{2,1,0:T(4,128)S(1)} fusion(f32[32,128]{0,1:T(8,128)S(1)} %get-tuple-element.1112, f32[32,128]{0,1:T(8,128)S(1)} %get-tuple-element.1113, f32[129,32,128]{0,1,2:T(8,128)} %multiply_exponential_fusion.3, f32[129,32,128]{0,1,2:T(8,128)} %iota_multiply_fusion.3, f32[1,4,32,128]{2,1,3,0:T(4,128)S(1)} %copy.94, ...), kind=kOutput, calls=%fused_computation.10.clone.1 | convolution fusion | flops 15269888 | bytes 4718592 | tf_op jit(solution)/shard_map/while/body/eval_jaxpr/tns,bns->bts/dot_general | solution.py:128
  515.1 11.8 %fusion.173 = bf16[4,128,128]{1,0,2:T(4,128)(2,1)S(1)} fusion(f32[4,128,128]{1,0,2:T(4,128)S(1)} %copy.93, f32[128,4,128]{2,1,0:T(4,128)S(1)} %fusion.171, f32[32,128]{0,1:T(8,128)S(1)} %get-tuple-element.1112, f32[32,128]{0,1:T(8,128)S(1)} %get-tuple-element.1113, f32[129,32,128]{0,1,2:T(8,128)} %iota_multiply_fusion.3, ...), kind=kOutput, calls=%fused_computation.37.clone.1 | convolution fusion | flops 16187392 | bytes 5374464 | tf_op jit(solution)/shard_map/while/body/eval_jaxpr/tns,bns->bts/dot_general | solution.py:127
  536.7 11.6 %fusion.171 = f32[128,4,128]{2,1,0:T(4,128)S(1)} fusion(f32[32,128]{0,1:T(8,128)S(1)} %get-tuple-element.1112, f32[32,128]{0,1:T(8,128)S(1)} %get-tuple-element.1113, f32[129,32,128]{0,1,2:T(8,128)} %multiply_exponential_fusion.3, f32[129,32,128]{0,1,2:T(8,128)} %iota_multiply_fusion.3, f32[1,4,32,128]{2,1,3,0:T(4,128)S(1)} %copy.94, ...), kind=kOutput, calls=%fused_computation.10.clone.1 | convolution fusion | flops 15269888 | bytes 4718592 | tf_op jit(solution)/shard_map/while/body/eval_jaxpr/tns,bns->bts/dot_general | solution.py:128
  551.3 11.8 %fusion.173 = bf16[4,128,128]{1,0,2:T(4,128)(2,1)S(1)} fusion(f32[4,128,128]{1,0,2:T(4,128)S(1)} %copy.93, f32[128,4,128]{2,1,0:T(4,128)S(1)} %fusion.171, f32[32,128]{0,1:T(8,128)S(1)} %get-tuple-element.1112, f32[32,128]{0,1:T(8,128)S(1)} %get-tuple-element.1113, f32[129,32,128]{0,1,2:T(8,128)} %iota_multiply_fusion.3, ...), kind=kOutput, calls=%fused_computation.37.clone.1 | convolution fusion | flops 16187392 | bytes 5374464 | tf_op jit(solution)/shard_map/while/body/eval_jaxpr/tns,bns->bts/dot_general | solution.py:127
  573.0 11.6 %fusion.171 = f32[128,4,128]{2,1,0:T(4,128)S(1)} fusion(f32[32,128]{0,1:T(8,128)S(1)} %get-tuple-element.1112, f32[32,128]{0,1:T(8,128)S(1)} %get-tuple-element.1113, f32[129,32,128]{0,1,2:T(8,128)} %multiply_exponential_fusion.3, f32[129,32,128]{0,1,2:T(8,128)} %iota_multiply_fusion.3, f32[1,4,32,128]{2,1,3,0:T(4,128)S(1)} %copy.94, ...), kind=kOutput, calls=%fused_computation.10.clone.1 | convolution fusion | flops 15269888 | bytes 4718592 | tf_op jit(solution)/shard_map/while/body/eval_jaxpr/tns,bns->bts/dot_general | solution.py:128
  587.5 11.8 %fusion.173 = bf16[4,128,128]{1,0,2:T(4,128)(2,1)S(1)} fusion(f32[4,128,128]{1,0,2:T(4,128)S(1)} %copy.93, f32[128,4,128]{2,1,0:T(4,128)S(1)} %fusion.171, f32[32,128]{0,1:T(8,128)S(1)} %get-tuple-element.1112, f32[32,128]{0,1:T(8,128)S(1)} %get-tuple-element.1113, f32[129,32,128]{0,1,2:T(8,128)} %iota_multiply_fusion.3, ...), kind=kOutput, calls=%fused_computation.37.clone.1 | convolution fusion | flops 16187392 | bytes 5374464 | tf_op jit(solution)/shard_map/while/body/eval_jaxpr/tns,bns->bts/dot_general | solution.py:127
  609.2 11.6 %fusion.171 = f32[128,4,128]{2,1,0:T(4,128)S(1)} fusion(f32[32,128]{0,1:T(8,128)S(1)} %get-tuple-element.1112, f32[32,128]{0,1:T(8,128)S(1)} %get-tuple-element.1113, f32[129,32,128]{0,1,2:T(8,128)} %multiply_exponential_fusion.3, f32[129,32,128]{0,1,2:T(8,128)} %iota_multiply_fusion.3, f32[1,4,32,128]{2,1,3,0:T(4,128)S(1)} %copy.94, ...), kind=kOutput, calls=%fused_computation.10.clone.1 | convolution fusion | flops 15269888 | bytes 4718592 | tf_op jit(solution)/shard_map/while/body/eval_jaxpr/tns,bns->bts/dot_general | solution.py:128
  623.8 11.8 %fusion.173 = bf16[4,128,128]{1,0,2:T(4,128)(2,1)S(1)} fusion(f32[4,128,128]{1,0,2:T(4,128)S(1)} %copy.93, f32[128,4,128]{2,1,0:T(4,128)S(1)} %fusion.171, f32[32,128]{0,1:T(8,128)S(1)} %get-tuple-element.1112, f32[32,128]{0,1:T(8,128)S(1)} %get-tuple-element.1113, f32[129,32,128]{0,1,2:T(8,128)} %iota_multiply_fusion.3, ...), kind=kOutput, calls=%fused_computation.37.clone.1 | convolution fusion | flops 16187392 | bytes 5374464 | tf_op jit(solution)/shard_map/while/body/eval_jaxpr/tns,bns->bts/dot_general | solution.py:127
  645.4 11.6 %fusion.171 = f32[128,4,128]{2,1,0:T(4,128)S(1)} fusion(f32[32,128]{0,1:T(8,128)S(1)} %get-tuple-element.1112, f32[32,128]{0,1:T(8,128)S(1)} %get-tuple-element.1113, f32[129,32,128]{0,1,2:T(8,128)} %multiply_exponential_fusion.3, f32[129,32,128]{0,1,2:T(8,128)} %iota_multiply_fusion.3, f32[1,4,32,128]{2,1,3,0:T(4,128)S(1)} %copy.94, ...), kind=kOutput, calls=%fused_computation.10.clone.1 | convolution fusion | flops 15269888 | bytes 4718592 | tf_op jit(solution)/shard_map/while/body/eval_jaxpr/tns,bns->bts/dot_general | solution.py:128
  660.0 11.8 %fusion.173 = bf16[4,128,128]{1,0,2:T(4,128)(2,1)S(1)} fusion(f32[4,128,128]{1,0,2:T(4,128)S(1)} %copy.93, f32[128,4,128]{2,1,0:T(4,128)S(1)} %fusion.171, f32[32,128]{0,1:T(8,128)S(1)} %get-tuple-element.1112, f32[32,128]{0,1:T(8,128)S(1)} %get-tuple-element.1113, f32[129,32,128]{0,1,2:T(8,128)} %iota_multiply_fusion.3, ...), kind=kOutput, calls=%fused_computation.37.clone.1 | convolution fusion | flops 16187392 | bytes 5374464 | tf_op jit(solution)/shard_map/while/body/eval_jaxpr/tns,bns->bts/dot_general | solution.py:127
  672.5 54.2 %all-gather.11.cloned.1.call-done = bf16[512,3072]{0,1:T(8,128)(2,1)} async-done(((bf16[512,768]{0,1:T(8,128)(2,1)}), bf16[512,3072]{0,1:T(8,128)(2,1)}) %all-gather.11.cloned.1.call-update) | async-done | bytes 3145744 | tf_op jit(solution)/shard_map/all_gather | solution.py:185
  726.8 6.8 add_convert_fusion
  (668 shorter events, 280.8 us)
Async XLA Ops:
  6.5 289.7 %all-gather.15.cloned.1.call-start = ((), (), s32[]{:S(2)}) async-start(), calls=%async_computation.2 | async-start | bytes 3244032 | tf_op jit(solution)/shard_map/all_gather | solution.py:16
  8.1 3.3 copy-start.4
  12.7 7.7 %copy-start.13 = (f32[6,32,128]{2,1,0:T(8,128)}, f32[6,32,128]{2,1,0:T(8,128)S(1)}, u32[]{:S(2)}) copy-start(f32[6,32,128]{2,1,0:T(8,128)S(1)} %get-tuple-element.1238) | copy-start | bytes 294916 | tf_op jit(solution)/shard_map/while
  12.7 7.7 %copy-start.15 = (f32[6,32,128]{2,1,0:T(8,128)}, f32[6,32,128]{2,1,0:T(8,128)S(1)}, u32[]{:S(2)}) copy-start(f32[6,32,128]{2,1,0:T(8,128)S(1)} %get-tuple-element.1239) | copy-start | bytes 294916 | tf_op jit(solution)/shard_map/while
  12.7 7.7 %copy-start.11 = (f32[6,32,128]{2,1,0:T(8,128)}, f32[6,32,128]{2,1,0:T(8,128)S(1)}, u32[]{:S(2)}) copy-start(f32[6,32,128]{2,1,0:T(8,128)S(1)} %get-tuple-element.1240) | copy-start | bytes 294916 | tf_op jit(solution)/shard_map/while
  12.7 7.7 %copy-start.9 = (f32[6,32,128]{2,1,0:T(8,128)}, f32[6,32,128]{2,1,0:T(8,128)S(1)}, u32[]{:S(2)}) copy-start(f32[6,32,128]{2,1,0:T(8,128)S(1)} %get-tuple-element.1237) | copy-start | bytes 294916 | tf_op jit(solution)/shard_map/while
  52.1 7.7 %copy-start.13 = (f32[6,32,128]{2,1,0:T(8,128)}, f32[6,32,128]{2,1,0:T(8,128)S(1)}, u32[]{:S(2)}) copy-start(f32[6,32,128]{2,1,0:T(8,128)S(1)} %get-tuple-element.1238) | copy-start | bytes 294916 | tf_op jit(solution)/shard_map/while
  52.1 7.7 %copy-start.15 = (f32[6,32,128]{2,1,0:T(8,128)}, f32[6,32,128]{2,1,0:T(8,128)S(1)}, u32[]{:S(2)}) copy-start(f32[6,32,128]{2,1,0:T(8,128)S(1)} %get-tuple-element.1239) | copy-start | bytes 294916 | tf_op jit(solution)/shard_map/while
  52.1 7.7 %copy-start.11 = (f32[6,32,128]{2,1,0:T(8,128)}, f32[6,32,128]{2,1,0:T(8,128)S(1)}, u32[]{:S(2)}) copy-start(f32[6,32,128]{2,1,0:T(8,128)S(1)} %get-tuple-element.1240) | copy-start | bytes 294916 | tf_op jit(solution)/shard_map/while
  52.1 7.7 %copy-start.9 = (f32[6,32,128]{2,1,0:T(8,128)}, f32[6,32,128]{2,1,0:T(8,128)S(1)}, u32[]{:S(2)}) copy-start(f32[6,32,128]{2,1,0:T(8,128)S(1)} %get-tuple-element.1237) | copy-start | bytes 294916 | tf_op jit(solution)/shard_map/while
  91.5 7.7 %copy-start.13 = (f32[6,32,128]{2,1,0:T(8,128)}, f32[6,32,128]{2,1,0:T(8,128)S(1)}, u32[]{:S(2)}) copy-start(f32[6,32,128]{2,1,0:T(8,128)S(1)} %get-tuple-element.1238) | copy-start | bytes 294916 | tf_op jit(solution)/shard_map/while
  91.5 7.7 %copy-start.15 = (f32[6,32,128]{2,1,0:T(8,128)}, f32[6,32,128]{2,1,0:T(8,128)S(1)}, u32[]{:S(2)}) copy-start(f32[6,32,128]{2,1,0:T(8,128)S(1)} %get-tuple-element.1239) | copy-start | bytes 294916 | tf_op jit(solution)/shard_map/while
  91.5 7.7 %copy-start.11 = (f32[6,32,128]{2,1,0:T(8,128)}, f32[6,32,128]{2,1,0:T(8,128)S(1)}, u32[]{:S(2)}) copy-start(f32[6,32,128]{2,1,0:T(8,128)S(1)} %get-tuple-element.1240) | copy-start | bytes 294916 | tf_op jit(solution)/shard_map/while
  91.6 7.7 %copy-start.9 = (f32[6,32,128]{2,1,0:T(8,128)}, f32[6,32,128]{2,1,0:T(8,128)S(1)}, u32[]{:S(2)}) copy-start(f32[6,32,128]{2,1,0:T(8,128)S(1)} %get-tuple-element.1237) | copy-start | bytes 294916 | tf_op jit(solution)/shard_map/while
  131.0 7.7 %copy-start.13 = (f32[6,32,128]{2,1,0:T(8,128)}, f32[6,32,128]{2,1,0:T(8,128)S(1)}, u32[]{:S(2)}) copy-start(f32[6,32,128]{2,1,0:T(8,128)S(1)} %get-tuple-element.1238) | copy-start | bytes 294916 | tf_op jit(solution)/shard_map/while
  131.0 7.7 %copy-start.15 = (f32[6,32,128]{2,1,0:T(8,128)}, f32[6,32,128]{2,1,0:T(8,128)S(1)}, u32[]{:S(2)}) copy-start(f32[6,32,128]{2,1,0:T(8,128)S(1)} %get-tuple-element.1239) | copy-start | bytes 294916 | tf_op jit(solution)/shard_map/while
  131.0 7.7 %copy-start.11 = (f32[6,32,128]{2,1,0:T(8,128)}, f32[6,32,128]{2,1,0:T(8,128)S(1)}, u32[]{:S(2)}) copy-start(f32[6,32,128]{2,1,0:T(8,128)S(1)} %get-tuple-element.1240) | copy-start | bytes 294916 | tf_op jit(solution)/shard_map/while
  131.0 7.7 %copy-start.9 = (f32[6,32,128]{2,1,0:T(8,128)}, f32[6,32,128]{2,1,0:T(8,128)S(1)}, u32[]{:S(2)}) copy-start(f32[6,32,128]{2,1,0:T(8,128)S(1)} %get-tuple-element.1237) | copy-start | bytes 294916 | tf_op jit(solution)/shard_map/while
  170.4 7.7 %copy-start.13 = (f32[6,32,128]{2,1,0:T(8,128)}, f32[6,32,128]{2,1,0:T(8,128)S(1)}, u32[]{:S(2)}) copy-start(f32[6,32,128]{2,1,0:T(8,128)S(1)} %get-tuple-element.1238) | copy-start | bytes 294916 | tf_op jit(solution)/shard_map/while
  170.4 7.7 %copy-start.15 = (f32[6,32,128]{2,1,0:T(8,128)}, f32[6,32,128]{2,1,0:T(8,128)S(1)}, u32[]{:S(2)}) copy-start(f32[6,32,128]{2,1,0:T(8,128)S(1)} %get-tuple-element.1239) | copy-start | bytes 294916 | tf_op jit(solution)/shard_map/while
  170.4 7.7 %copy-start.11 = (f32[6,32,128]{2,1,0:T(8,128)}, f32[6,32,128]{2,1,0:T(8,128)S(1)}, u32[]{:S(2)}) copy-start(f32[6,32,128]{2,1,0:T(8,128)S(1)} %get-tuple-element.1240) | copy-start | bytes 294916 | tf_op jit(solution)/shard_map/while
  170.4 7.7 %copy-start.9 = (f32[6,32,128]{2,1,0:T(8,128)}, f32[6,32,128]{2,1,0:T(8,128)S(1)}, u32[]{:S(2)}) copy-start(f32[6,32,128]{2,1,0:T(8,128)S(1)} %get-tuple-element.1237) | copy-start | bytes 294916 | tf_op jit(solution)/shard_map/while
  209.9 7.7 %copy-start.13 = (f32[6,32,128]{2,1,0:T(8,128)}, f32[6,32,128]{2,1,0:T(8,128)S(1)}, u32[]{:S(2)}) copy-start(f32[6,32,128]{2,1,0:T(8,128)S(1)} %get-tuple-element.1238) | copy-start | bytes 294916 | tf_op jit(solution)/shard_map/while
  209.9 7.7 %copy-start.15 = (f32[6,32,128]{2,1,0:T(8,128)}, f32[6,32,128]{2,1,0:T(8,128)S(1)}, u32[]{:S(2)}) copy-start(f32[6,32,128]{2,1,0:T(8,128)S(1)} %get-tuple-element.1239) | copy-start | bytes 294916 | tf_op jit(solution)/shard_map/while
  209.9 7.7 %copy-start.11 = (f32[6,32,128]{2,1,0:T(8,128)}, f32[6,32,128]{2,1,0:T(8,128)S(1)}, u32[]{:S(2)}) copy-start(f32[6,32,128]{2,1,0:T(8,128)S(1)} %get-tuple-element.1240) | copy-start | bytes 294916 | tf_op jit(solution)/shard_map/while
  209.9 7.7 %copy-start.9 = (f32[6,32,128]{2,1,0:T(8,128)}, f32[6,32,128]{2,1,0:T(8,128)S(1)}, u32[]{:S(2)}) copy-start(f32[6,32,128]{2,1,0:T(8,128)S(1)} %get-tuple-element.1237) | copy-start | bytes 294916 | tf_op jit(solution)/shard_map/while
  249.5 93.4 %all-gather.17.cloned.1.call-start = ((), (), s32[]{:S(2)}) async-start(), calls=%async_computation.3 | async-start | bytes 3244032 | tf_op jit(solution)/shard_map/all_gather | solution.py:16
  250.3 139.4 %all-gather.19.cloned.1.call-start = ((), (), s32[]{:S(2)}) async-start(), calls=%async_computation.4 | async-start | bytes 3244032 | tf_op jit(solution)/shard_map/all_gather | solution.py:16
  251.0 185.3 %all-gather.21.cloned.1.call-start = ((), (), s32[]{:S(2)}) async-start(), calls=%async_computation.5 | async-start | bytes 3244032 | tf_op jit(solution)/shard_map/all_gather | solution.py:16
  251.6 421.0 %all-gather.13.cloned.1.call-start = ((), (), s32[]{:S(2)}) async-start(), calls=%async_computation.1 | async-start | bytes 4866048 | tf_op jit(solution)/shard_map/all_gather | solution.py:188
  252.2 474.6 %all-gather.11.cloned.1.call-start = ((), (), s32[]{:S(2)}) async-start(), calls=%async_computation | async-start | bytes 3932160 | tf_op jit(solution)/shard_map/all_gather | solution.py:185
  454.9 271.9 %copy-start.8 = (bf16[512,768]{1,0:T(8,128)(2,1)S(1)}, bf16[512,768]{1,0:T(8,128)(2,1)}, u32[]{:S(2)}) copy-start(bf16[512,768]{1,0:T(8,128)(2,1)} %param.14) | copy-start | bytes 2359300
  (48 other events, 100.5 us)
Sparse Core Ops, SparseCore 0:
  249.6 46.5 all-gather.14
  298.4 44.4 all-gather.16
  345.2 44.4 all-gather.18
  391.8 44.4 all-gather.20
  438.4 45.9 all-gather.12
  672.6 54.0 all-gather.10
where the time goes:
time: 748 us; the launch traced here: 740 us
  waiting for transfers between devices  241 us (32%)
  matrix products  201 us (27%)
  local copies, waits for them, and re-layouts  144 us (19%)
  other arithmetic  137 us (18%)
  between operations  13.6 us (2%)
    all_gather x4, waiting for transfers between devices, entering(): gathered = jax.tree.map(lambda a: lax.all_gather(a, axis), part)  184 us
    dot_general x6, matrix products, finish_slab(): jnp.einsum('tns,bns->bts', outer_re, full_re, precision=three_pass)  70.7 us
    dot_general x6, matrix products, finish_slab(): jnp.einsum('tns,bns->bts', outer_im, full_im, precision=three_pass)  69.5 us
    all_gather x1, waiting for transfers between devices, local(): gathered = lax.all_gather(act, 'chan', axis=1, tiled=True)  54.2 us
    mul x6, other arithmetic, mode_powers(): return (magnitude * jnp.cos(turned), magnitude * jnp.sin(turned))  45.7 us
    dot_general x18, matrix products, split_product(): first = jnp.einsum(form, upper, data, preferred_element_type=jnp.float32)  32.3 us
    convert_element_type x12, local copies, waits for them, and re-layouts, split_product(): upper = table.astype(jnp.bfloat16)  28.1 us
    convert_element_type x12, local copies, waits for them, and re-layouts, split_product(): lower = (table - upper.astype(jnp.float32)).astype(jnp.bfloat16)  23.2 us
  transfers between devices with their start and end apart: 6, of which 5 were waited for; matrix products, arithmetic and copies ran while one was open for 32% of the time, Pallas kernels for 0%

commit v1 on v0

v1 whole, which is shorter than its diff:
```python
import jax
import jax.numpy as jnp
from jax import lax
from jax.experimental import pallas as pl
from jax.experimental.pallas import tpu as pltpu
from jax.sharding import PartitionSpec as P

BLK = 32
LANES = 128
GROUP = 4

f32 = jnp.float32
bf16 = jnp.bfloat16


def cmul(ar, ai, br, bi):
    return ar * br - ai * bi, ar * bi + ai * br


def decay(rates_ref, freqs_ref):
    size = jnp.exp(-rates_ref[...])
    angle = freqs_ref[...]
    return size * jnp.cos(angle), size * jnp.sin(angle)


def ends_kernel(u_ref, r_ref, f_ref, part_ref, end_ref, send_ref, step_ref, whole_ref, uf, table):
    uf[...] = u_ref[...].astype(f32)
    lr, li = decay(r_ref, f_ref)
    powers = [(jnp.ones_like(lr), jnp.zeros_like(lr)), (lr, li)]
    for j in range(2, BLK + 1):
        half = powers[j // 2]
        powers.append(cmul(*half, *powers[j - j // 2]))
    for j in range(BLK):
        table[j, 0] = powers[j][0]
        table[j, 1] = powers[j][1]
    sr, si = powers[BLK]
    step_ref[0] = sr
    step_ref[1] = si
    wr, wi = sr, si
    count = BLK
    while count < u_ref.shape[0]:
        wr, wi = cmul(wr, wi, wr, wi)
        count *= 2
    whole_ref[0] = wr
    whole_ref[1] = wi

    def group(g, end):
        er, ei = end
        accs = [[jnp.zeros_like(lr), jnp.zeros_like(lr)] for _ in range(GROUP)]
        for b in range(BLK):
            tr = table[BLK - 1 - b, 0]
            ti = table[BLK - 1 - b, 1]
            for i in range(GROUP):
                row = uf[pl.ds((g * GROUP + i) * BLK + b, 1), :]
                accs[i][0] += tr * row
                accs[i][1] += ti * row
        for i in range(GROUP):
            part_ref[g * GROUP + i, 0] = accs[i][0]
            part_ref[g * GROUP + i, 1] = accs[i][1]
            er, ei = cmul(er, ei, sr, si)
            er = er + accs[i][0]
            ei = ei + accs[i][1]
        return er, ei

    er, ei = lax.fori_loop(
        0, u_ref.shape[0] // BLK // GROUP, group, (jnp.zeros_like(lr), jnp.zeros_like(lr))
    )
    end_ref[0] = er
    end_ref[1] = ei
    send_ref[0] = er.astype(bf16)
    send_ref[1] = ei.astype(bf16)


def inner_kernel(u_ref, r_ref, f_ref, c_ref, skip_ref, coef_ref, base_ref, pad, rows, taps):
    modes = r_ref.shape[0]
    lr, li = decay(r_ref, f_ref)
    q2 = cmul(lr, li, lr, li)
    q4 = cmul(*q2, *q2)
    q8 = cmul(*q4, *q4)
    cr = 2.0 * c_ref[0]
    ci = 2.0 * c_ref[1]
    first = cmul(cr, ci, lr, li)
    for k, pair in enumerate((first, (lr, li), q2, q4, q8)):
        rows[2 * k] = pair[0]
        rows[2 * k + 1] = pair[1]
    place = lax.broadcasted_iota(jnp.int32, (8, LANES), 0)
    bits = [(place & (1 << k)) != 0 for k in range(3)]

    def mode(n, sums):
        row = [jnp.broadcast_to(rows[k, pl.ds(n, 1), :], (8, LANES)) for k in range(10)]
        vr, vi = row[0], row[1]
        for k in range(3):
            nr, ni = cmul(vr, vi, row[2 + 2 * k], row[3 + 2 * k])
            vr = jnp.where(bits[k], nr, vr)
            vi = jnp.where(bits[k], ni, vi)
        out = []
        for i in range(BLK // 8):
            coef_ref[n, 0, 8 * i : 8 * i + 8] = vr
            coef_ref[n, 1, 8 * i : 8 * i + 8] = -vi
            out.append(sums[i] + vr)
            if i + 1 < BLK // 8:
                vr, vi = cmul(vr, vi, row[8], row[9])
        return tuple(out)

    zero = jnp.zeros((8, LANES), f32)
    sums = lax.fori_loop(0, modes, mode, (zero,) * (BLK // 8), unroll=2)
    taps[0:1] = jnp.sum(cr, axis=0, keepdims=True) + skip_ref[...]
    for i in range(BLK // 8):
        taps[8 * i + 1 : 8 * i + 9] = sums[i]
    blocks = u_ref.shape[0] // BLK
    pad[:, 0:8] = jnp.zeros((blocks, 8, LANES), f32)
    pad[:, 8:] = u_ref[...].astype(f32).reshape(blocks, BLK, LANES)

    def group(g, _):
        accs = [[zero] * (BLK // 8) for _ in range(GROUP)]
        for j in range(BLK):
            tap = jnp.broadcast_to(taps[j : j + 1], (8, LANES))
            for i in range(BLK // 8):
                if 8 * i + 7 >= j:
                    for k in range(GROUP):
                        accs[k][i] += tap * pad[g * GROUP + k, 8 + 8 * i - j : 16 + 8 * i - j]
        for k in range(GROUP):
            for i in range(BLK // 8):
                base_ref[pl.ds((g * GROUP + k) * BLK + 8 * i, 8), :] = accs[k][i]
        return 0

    lax.fori_loop(0, blocks // GROUP, group, 0)


def finish_kernel(part_ref, step_ref, coef_ref, base_ref, own_ref, w_ref, q1_ref, q2_ref, q3_ref, act_ref, held):
    hr = own_ref[0]
    hi = own_ref[1]
    for k, q in enumerate((q1_ref, q2_ref, q3_ref)):
        ar, ai = cmul(w_ref[k, 0], w_ref[k, 1], q[0].astype(f32), q[1].astype(f32))
        hr = hr + ar
        hi = hi + ai
    sr = step_ref[0]
    si = step_ref[1]
    blocks = part_ref.shape[0]
    modes = hr.shape[0]
    for a in range(blocks):
        held[a, 0] = hr
        held[a, 1] = hi
        if a + 1 < blocks:
            hr, hi = cmul(hr, hi, sr, si)
            hr = hr + part_ref[a, 0]
            hi = hi + part_ref[a, 1]
    many = 8

    def group(g, _):
        accs = tuple(base_ref[pl.ds((g * many + k) * BLK, BLK), :] for k in range(many))

        def mode(n, accs):
            cr = coef_ref[n, 0]
            ci = coef_ref[n, 1]
            return tuple(
                accs[k]
                + (
                    cr * held[g * many + k, 0, pl.ds(n, 1), :]
                    + ci * held[g * many + k, 1, pl.ds(n, 1), :]
                )
                for k in range(many)
            )

        accs = lax.fori_loop(0, modes, mode, accs, unroll=4)
        for k in range(many):
            act_ref[pl.ds((g * many + k) * BLK, BLK), :] = jax.nn.gelu(accs[k]).astype(bf16)
        return 0

    lax.fori_loop(0, blocks // many, group, 0)


def params(limit=48):
    return pltpu.CompilerParams(vmem_limit_bytes=limit << 20)


def ends(signal, rates, freqs):
    tokens, channels = signal.shape
    modes = rates.shape[0]
    blocks = tokens // BLK
    pair = pl.BlockSpec((2, modes, LANES), lambda i: (0, 0, i))
    return pl.pallas_call(
        ends_kernel,
        grid=(channels // LANES,),
        in_specs=[
            pl.BlockSpec((tokens, LANES), lambda i: (0, i)),
            pl.BlockSpec((modes, LANES), lambda i: (0, i)),
            pl.BlockSpec((modes, LANES), lambda i: (0, i)),
        ],
        out_specs=[
            pl.BlockSpec((blocks, 2, modes, LANES), lambda i: (0, 0, 0, i)),
            pair,
            pair,
            pair,
            pair,
        ],
        out_shape=[
            jax.ShapeDtypeStruct((blocks, 2, modes, channels), f32),
            jax.ShapeDtypeStruct((2, modes, channels), f32),
            jax.ShapeDtypeStruct((2, modes, channels), bf16),
            jax.ShapeDtypeStruct((2, modes, channels), f32),
            jax.ShapeDtypeStruct((2, modes, channels), f32),
        ],
        scratch_shapes=[
            pltpu.VMEM((tokens, LANES), f32),
            pltpu.VMEM((BLK, 2, modes, LANES), f32),
        ],
        compiler_params=params(),
        cost_estimate=pl.CostEstimate(flops=10**9, bytes_accessed=6 * 10**6, transcendentals=0),
    )(signal, rates, freqs)


def inner(signal, rates, freqs, coeffs, skip):
    tokens, channels = signal.shape
    modes = rates.shape[0]
    blocks = tokens // BLK
    return pl.pallas_call(
        inner_kernel,
        grid=(channels // LANES,),
        in_specs=[
            pl.BlockSpec((tokens, LANES), lambda i: (0, i)),
            pl.BlockSpec((modes, LANES), lambda i: (0, i)),
            pl.BlockSpec((modes, LANES), lambda i: (0, i)),
            pl.BlockSpec((2, modes, LANES), lambda i: (0, 0, i)),
            pl.BlockSpec((1, LANES), lambda i: (0, i)),
        ],
        out_specs=[
            pl.BlockSpec((modes, 2, BLK, LANES), lambda i: (0, 0, 0, i)),
            pl.BlockSpec((tokens, LANES), lambda i: (0, i)),
        ],
        out_shape=[
            jax.ShapeDtypeStruct((modes, 2, BLK, channels), f32),
            jax.ShapeDtypeStruct((tokens, channels), f32),
        ],
        scratch_shapes=[
            pltpu.VMEM((blocks, BLK + 8, LANES), f32),
            pltpu.VMEM((10, modes, LANES), f32),
            pltpu.VMEM((BLK + 8, LANES), f32),
        ],
        compiler_params=params(),
        cost_estimate=pl.CostEstimate(flops=5 * 10**8, bytes_accessed=8 * 10**6, transcendentals=0),
    )(signal, rates, freqs, coeffs, skip.reshape(1, channels))


def finish(first, count, part, step, coef, base, own, weights, arrived):
    blocks, _, modes, _ = part.shape
    tokens = base.shape[0]
    pair = pl.BlockSpec((2, modes, LANES), lambda i: (0, 0, i + first))
    return pl.pallas_call(
        finish_kernel,
        grid=(count,),
        in_specs=[
            pl.BlockSpec((blocks, 2, modes, LANES), lambda i: (0, 0, 0, i + first)),
            pair,
            pl.BlockSpec((modes, 2, BLK, LANES), lambda i: (0, 0, 0, i + first)),
            pl.BlockSpec((tokens, LANES), lambda i: (0, i + first)),
            pair,
            pl.BlockSpec((3, 2, modes, LANES), lambda i: (0, 0, 0, i + first)),
            pair,
            pair,
            pair,
        ],
        out_specs=pl.BlockSpec((tokens, LANES), lambda i: (0, i)),
        out_shape=jax.ShapeDtypeStruct((tokens, count * LANES), bf16),
        scratch_shapes=[pltpu.VMEM((blocks, 2, modes, LANES), f32)],
        compiler_params=params(),
        cost_estimate=pl.CostEstimate(
            flops=10**9 // 6 * count, bytes_accessed=2 * 10**6 * count, transcendentals=0
        ),
    )(part, step, coef, base, own, weights, *arrived)


def times(a, b):
    ar, ai = a[0].astype(f32), a[1].astype(f32)
    br, bi = b[0].astype(f32), b[1].astype(f32)
    return jnp.stack([ar * br - ai * bi, ar * bi + ai * br])


def local(signal, rates, freqs, coeffs, skip, weight):
    wide = lax.all_gather(weight, "seq", axis=0, tiled=True)
    part, end, send, step, whole = ends(signal, rates, freqs)

    index = lax.axis_index("seq")
    x, z, c = index // 8, index // 2 % 4, index % 2
    core = [(i, i ^ 1) for i in range(32)]

    def along_z(k):
        return [(i, i // 8 * 8 + (i // 2 + k) % 4 * 2 + i % 2) for i in range(32)]

    def along_x(k):
        return [(i, (i + 8 * k) % 32) for i in range(32)]

    other = lax.ppermute(send, "seq", core).astype(f32)
    lower = jnp.where(c == 0, end, other)
    upper = jnp.where(c == 0, other, end)
    chip = (times(whole, lower) + upper).astype(bf16)

    unit = jnp.stack([jnp.ones_like(rates), jnp.zeros_like(rates)])
    p1 = times(whole, whole)
    p2 = times(p1, p1)
    p3 = times(p2, p1)
    p4 = times(p2, p2)
    p8 = times(p4, p4)
    chips = [unit, p1, p2, p3]

    def pick(k):
        return jnp.where(k == 0, unit, jnp.where(k == 1, p1, jnp.where(k == 2, p2, p3)))

    mine = jnp.where(c == 0, unit, whole)

    from_z = [lax.ppermute(chip, "seq", along_z(k)) for k in (1, 2, 3)]
    line = times(pick(3 - z), chip)
    for k in (1, 2, 3):
        line = line + times(pick(3 - (z - k) % 4), from_z[k - 1])
    line = line.astype(bf16)
    own = jnp.zeros_like(end)
    for k in (1, 2, 3):
        own = own + jnp.where(z >= k, times(chips[k - 1], from_z[k - 1]), 0.0)
    own = times(mine, own) + jnp.where(c == 1, lower, 0.0)

    from_x = [lax.ppermute(line, "seq", along_x(k)) for k in (1, 2, 3)]
    here = times(mine, pick(z))
    weights = jnp.stack(
        [
            jnp.where(x >= k, times(here, far), 0.0)
            for k, far in ((1, unit), (2, p4), (3, p8))
        ]
    )
    coef, base = inner(signal, rates, freqs, coeffs, skip)

    slabs = 2
    count = signal.shape[1] // LANES // slabs
    ring = lambda k: [(i, (i + k) % 4) for i in range(4)]
    half = signal.shape[0] // 2
    y = lax.axis_index("chan")
    width = count * LANES
    pieces = []
    for s in range(slabs):
        act = finish(s * count, count, part, step, coef, base, own, weights, from_x)
        up = lax.ppermute(act, "chan", ring(1))
        down = lax.ppermute(act, "chan", ring(3))
        far_up = lax.ppermute(up[:half], "chan", ring(1))
        far_down = lax.ppermute(down[half:], "chan", ring(3))
        pieces.append((act, up, down, jnp.concatenate([far_up, far_down])))
    total = signal.astype(f32)
    for k, off in enumerate((0, 3, 1, 2)):
        for s in range(slabs):
            rows = lax.dynamic_slice_in_dim(
                wide, (y + off) % 4 * signal.shape[1] + s * width, width, 0
            )
            total = total + jnp.dot(pieces[s][k], rows, preferred_element_type=f32)
    return total.astype(bf16)


def solution(mesh):
    in_specs = (
        P("seq", "chan"),
        P(None, "chan"),
        P(None, "chan"),
        P(None, None, "chan"),
        P("chan"),
        P("seq", "chan"),
    )
    return jax.shard_map(
        local, mesh=mesh, in_specs=in_specs, out_specs=P("seq", "chan"), check_vma=False
    )
```

time: 748 us -> 103 us (0.14)
  waiting for transfers between devices: 241 us -> 19.7 us
  matrix products: 201 us -> 9.95 us
  local copies, waits for them, and re-layouts: 144 us -> 6.1 us
  other arithmetic: 137 us -> 0.82 us
  Pallas kernels: 0 us -> 28.3 us
  starting transfers between devices: 0.2 us -> 22.6 us
    all_gather x6 -> x1, waiting for transfers between devices: 238 us -> 0.01 us  [local(): wide = lax.all_gather(weight, 'seq', axis=0, tiled=True)]
    dot_general x61 -> x8, matrix products: 201 us -> 9.95 us  [local(): total = total + jnp.dot(pieces[s][k], rows, preferred_element_type=f32)]
    mul x30 -> x0, other arithmetic: 67.6 us -> none  [the longest x6 45.7 us: mode_powers(): return (magnitude * jnp.cos(turned), magnitude * jnp.sin(turned))]
    convert_element_type x30 -> x0, local copies, waits for them, and re-layouts: 51.9 us -> none  [the longest x12 28.1 us: split_product(): upper = table.astype(jnp.bfloat16)]
    pallas_call x0 -> x4, Pallas kernels: none -> 28.3 us  [the longest x2 11.9 us: finish(): pl.pallas_call(finish_kernel, grid=(count,), in_specs=[pl.BlockSpec((bloc...]
    dynamic_slice x72 -> x0, local copies, waits for them, and re-layouts: 27.5 us -> none  [the longest x42 20 us: local(): lax.map(finish_slab, (slab_signal, slab_decay, slab_angle, slab_cre, slab...]
    dynamic_update_slice x36 -> x0, local copies, waits for them, and re-layouts: 23.8 us -> none  [the longest x30 19.8 us: local(): lax.map(local_slab, (slab_signal, slab_decay, slab_angle, slab_cre, slab_...]
    ppermute x0 -> x15, starting transfers between devices: none -> 22.6 us  [the longest x2 6.51 us: local(): far_up = lax.ppermute(up[:half], 'chan', ring(1))]
  transfers between devices with their start and end apart: 6 -> 16, of which waited for: 5 -> 6; matrix products, arithmetic and copies ran while one was open for 32% -> 9% of each run, Pallas kernels for 0% -> 28%
where the time goes in v1:
time: 103 us; the launch traced here: 101 us
  Pallas kernels  28.3 us (27%)
  starting transfers between devices  22.6 us (22%)
  waiting for transfers between devices  19.7 us (19%)
  between operations  13.8 us (13%)
  matrix products  9.95 us (10%)
  local copies, waits for them, and re-layouts  6.1 us (6%)
    pallas_call x2, Pallas kernels, finish(): pl.pallas_call(finish_kernel, grid=(count,), in_specs=[pl.BlockSpec((bloc...  11.9 us
    dot_general x8, matrix products, local(): total = total + jnp.dot(pieces[s][k], rows, preferred_element_type=f32)  9.95 us
    pallas_call x1, Pallas kernels, ends(): pl.pallas_call(ends_kernel, grid=(channels // LANES,), in_specs=[pl.Block...  9.27 us
    ppermute x3, waiting for transfers between devices, local(): from_x = [lax.ppermute(line, 'seq', along_x(k)) for k in (1, 2, 3)]  7.3 us
    pallas_call x1, Pallas kernels, inner(): pl.pallas_call(inner_kernel, grid=(channels // LANES,), in_specs=[pl.Bloc...  7.14 us
    ppermute x2, starting transfers between devices, local(): far_up = lax.ppermute(up[:half], 'chan', ring(1))  6.51 us
    ppermute x3, starting transfers between devices, local(): from_z = [lax.ppermute(chip, 'seq', along_z(k)) for k in (1, 2, 3)]  5.98 us
    ppermute x2, waiting for transfers between devices, local(): down = lax.ppermute(act, 'chan', ring(3))  5.97 us
  transfers between devices with their start and end apart: 16, of which 6 were waited for; matrix products, arithmetic and copies ran while one was open for 9% of the time, Pallas kernels for 28%

profile of v1, /device:TPU:28, one launch (start us, length us, event | category | flops | bytes accessed | tf_op | source)
XLA Modules:
  0.0 101.2 jit_solution(17767005896694404113)
XLA Ops:
  6.5 0.7 all-gather.2.cloned.1.call-update
  7.3 1.1 %copy-done.1 = bf16[512,768]{1,0:T(8,128)(2,1)S(1)} copy-done((bf16[512,768]{1,0:T(8,128)(2,1)S(1)}, bf16[512,768]{1,0:T(8,128)(2,1)}, u32[]{:S(2)}) %copy-start.1) | copy-done | bytes 786456
  8.4 0.9 copy-done.4
  9.3 0.9 copy-done.6
  10.2 9.3 %shard_map.64 = (f32[16,2,32,768]{3,2,1,0:T(8,128)S(1)}, f32[2,32,768]{2,1,0:T(8,128)S(1)}, bf16[2,32,768]{2,1,0:T(8,128)(2,1)S(1)}, f32[2,32,768]{2,1,0:T(8,128)S(1)}, f32[2,32,768]{2,1,0:T(8,128)S(1)}) custom-call(bf16[512,768]{1,0:T(8,128)(2,1)S(1)} %copy-done.1, f32[32,768]{1,0:T(8,128)S(1)} %copy-done.4, f32[32,768]{1,0:T(8,128)S(1)} %copy-done.6), custom_call_target="tpu_custom_call" | custom-call | flops 1000000000 | bytes 6000000 | tf_op jit(solution)/shard_map/pallas_call | solution.py:182
  19.5 1.7 %copy-done = f32[16,2,32,768]{3,2,1,0:T(8,128)} copy-done((f32[16,2,32,768]{3,2,1,0:T(8,128)}, f32[16,2,32,768]{3,2,1,0:T(8,128)S(1)}, u32[]{:S(2)}) %copy-start) | copy-done | bytes 3145752
  21.3 1.3 %collective-permute-done = bf16[2,32,768]{2,1,0:T(8,128)(2,1)S(1)} collective-permute-done((bf16[2,32,768]{2,1,0:T(8,128)(2,1)S(1)}, bf16[2,32,768]{2,1,0:T(8,128)(2,1)S(1)}, u32[]{:S(2)}, u32[]{:S(2)}) %collective-permute-start) | collective-permute-done | bytes 98336 | tf_op jit(solution)/shard_map/ppermute | solution.py:293
  22.7 4.0 %collective-permute-start.2 = (bf16[2,32,768]{2,1,0:T(8,128)(2,1)S(1)}, bf16[2,32,768]{2,1,0:T(8,128)(2,1)S(1)}, u32[]{:S(2)}, u32[]{:S(2)}) collective-permute-start(bf16[2,32,768]{2,1,0:T(8,128)(2,1)S(1)} %fusion.25), channel_id=1, source_target_pairs={{0,16},{4,20},{8,24},{12,28},{16,0},{20,4},{24,8},{28,12},{32,48},... | collective-permute-start | bytes 294920 | tf_op jit(solution)/shard_map/ppermute | solution.py:311
  26.7 7.1 %shard_map.65 = (f32[32,2,32,768]{3,2,1,0:T(8,128)}, f32[512,768]{1,0:T(8,128)S(1)}) custom-call(bf16[512,768]{1,0:T(8,128)(2,1)S(1)} %copy-done.2, f32[32,768]{1,0:T(8,128)S(1)} %copy-done.5, f32[32,768]{1,0:T(8,128)S(1)} %copy-done.7, f32[2,32,768]{2,1,0:T(8,128)S(1)} %copy-done.3, f32[1,768]{1,0:T(1,128)S(1)} %reshape.90.skip_ref), custom_call_target="tpu_custom_call" | custom-call | flops 500000000 | bytes 8000000 | tf_op jit(solution)/shard_map/pallas_call | solution.py:217
  33.9 0.7 collective-permute-start.3
  34.6 1.3 %collective-permute-start.1 = (bf16[2,32,768]{2,1,0:T(8,128)(2,1)S(1)}, bf16[2,32,768]{2,1,0:T(8,128)(2,1)S(1)}, u32[]{:S(2)}, u32[]{:S(2)}) collective-permute-start(bf16[2,32,768]{2,1,0:T(8,128)(2,1)S(1)} %fusion.25), channel_id=1, source_target_pairs={{0,8},{4,12},{8,16},{12,20},{16,24},{20,28},{24,0},{28,4},{32,40},... | collective-permute-start | bytes 294920 | tf_op jit(solution)/shard_map/ppermute | solution.py:311
  36.0 4.4 %collective-permute-done.1 = bf16[2,32,768]{2,1,0:T(8,128)(2,1)S(1)} collective-permute-done((bf16[2,32,768]{2,1,0:T(8,128)(2,1)S(1)}, bf16[2,32,768]{2,1,0:T(8,128)(2,1)S(1)}, u32[]{:S(2)}, u32[]{:S(2)}) %collective-permute-start.1) | collective-permute-done | bytes 98336 | tf_op jit(solution)/shard_map/ppermute | solution.py:311
  40.8 0.6 collective-permute-start.6
  41.5 2.7 %collective-permute-start.5 = (bf16[2,32,768]{2,1,0:T(8,128)(2,1)S(1)}, bf16[2,32,768]{2,1,0:T(8,128)(2,1)S(1)}, u32[]{:S(2)}, u32[]{:S(2)}) collective-permute-start(bf16[2,32,768]{2,1,0:T(8,128)(2,1)S(1)} %fusion.30), channel_id=1, source_target_pairs={{0,64},{4,68},{8,72},{12,76},{16,80},{20,84},{24,88},{28,92},{32,9... | collective-permute-start | bytes 294920 | tf_op jit(solution)/shard_map/ppermute | solution.py:321
  44.5 1.7 %collective-permute-done.6.q3_ref = bf16[2,32,768]{2,1,0:T(8,128)(2,1)S(1)} collective-permute-done((bf16[2,32,768]{2,1,0:T(8,128)(2,1)S(1)}, bf16[2,32,768]{2,1,0:T(8,128)(2,1)S(1)}, u32[]{:S(2)}, u32[]{:S(2)}) %collective-permute-start.6) | collective-permute-done | bytes 98336 | tf_op jit(solution)/shard_map/ppermute | solution.py:321
  46.1 3.9 %collective-permute-done.5.q2_ref = bf16[2,32,768]{2,1,0:T(8,128)(2,1)S(1)} collective-permute-done((bf16[2,32,768]{2,1,0:T(8,128)(2,1)S(1)}, bf16[2,32,768]{2,1,0:T(8,128)(2,1)S(1)}, u32[]{:S(2)}, u32[]{:S(2)}) %collective-permute-start.5) | collective-permute-done | bytes 98336 | tf_op jit(solution)/shard_map/ppermute | solution.py:321
  50.0 1.7 %collective-permute-done.4.q1_ref = bf16[2,32,768]{2,1,0:T(8,128)(2,1)S(1)} collective-permute-done((bf16[2,32,768]{2,1,0:T(8,128)(2,1)S(1)}, bf16[2,32,768]{2,1,0:T(8,128)(2,1)S(1)}, u32[]{:S(2)}, u32[]{:S(2)}) %collective-permute-start.4) | collective-permute-done | bytes 98336 | tf_op jit(solution)/shard_map/ppermute | solution.py:321
  51.8 6.0 %shard_map.66 = bf16[512,384]{1,0:T(8,128)(2,1)S(1)} custom-call(f32[16,2,32,768]{3,2,1,0:T(8,128)} %copy-done, f32[2,32,768]{2,1,0:T(8,128)S(1)} %get-tuple-element.13.step_ref, f32[32,2,32,768]{3,2,1,0:T(8,128)} %get-tuple-element.14.coef_ref, f32[512,768]{1,0:T(8,128)S(1)} %get-tuple-element.15.base_ref, f32[2,32,768]{2,1,0:T(8,128)S(1)} %maximum_add_fusion.own_ref, ...), custom_call_target="tpu_custom_call" | custom-call | flops 500000000 | bytes 6000000 | tf_op jit(solution)/shard_map/pallas_call | solution.py:249
  57.8 0.8 collective-permute-start.9
  58.5 2.5 %collective-permute-start.7 = (bf16[512,384]{1,0:T(8,128)(2,1)S(1)}, bf16[512,384]{1,0:T(8,128)(2,1)S(1)}, u32[]{:S(2)}, u32[]{:S(2)}) collective-permute-start(bf16[512,384]{1,0:T(8,128)(2,1)S(1)} %shard_map.66), channel_id=1, source_target_pairs={{0,1},{1,2},{2,3},{3,0},{4,5},{5,6},{6,7},{7,4},{8,9},{9,10},{10,1... | collective-permute-start | bytes 1179656 | tf_op jit(solution)/shard_map/ppermute | solution.py:340
  61.1 5.9 %shard_map.67 = bf16[512,384]{1,0:T(8,128)(2,1)S(1)} custom-call(f32[16,2,32,768]{3,2,1,0:T(8,128)} %copy-done, f32[2,32,768]{2,1,0:T(8,128)S(1)} %get-tuple-element.13.step_ref, f32[32,2,32,768]{3,2,1,0:T(8,128)} %get-tuple-element.14.coef_ref, f32[512,768]{1,0:T(8,128)S(1)} %get-tuple-element.15.base_ref, f32[2,32,768]{2,1,0:T(8,128)S(1)} %maximum_add_fusion.own_ref, ...), custom_call_target="tpu_custom_call" | custom-call | flops 500000000 | bytes 6000000 | tf_op jit(solution)/shard_map/pallas_call | solution.py:249
  67.1 3.2 %collective-permute-start.8 = (bf16[512,384]{1,0:T(8,128)(2,1)S(1)}, bf16[512,384]{1,0:T(8,128)(2,1)S(1)}, u32[]{:S(2)}, u32[]{:S(2)}) collective-permute-start(bf16[512,384]{1,0:T(8,128)(2,1)S(1)} %shard_map.67), channel_id=1, source_target_pairs={{0,1},{1,2},{2,3},{3,0},{4,5},{5,6},{6,7},{7,4},{8,9},{9,10},{10,1... | collective-permute-start | bytes 1179656 | tf_op jit(solution)/shard_map/ppermute | solution.py:340
  70.5 3.3 %collective-permute-start.11 = (bf16[256,384]{1,0:T(8,128)(2,1)S(1)}, bf16[256,384]{1,0:T(8,128)(2,1)}, u32[]{:S(2)}, u32[]{:S(2)}) collective-permute-start(bf16[256,384]{1,0:T(8,128)(2,1)S(1)} %slice.156), channel_id=1, source_target_pairs={{0,1},{1,2},{2,3},{3,0},{4,5},{5,6},{6,7},{7,4},{8,9},{9,10},{10,1... | collective-permute-start | bytes 589832 | tf_op jit(solution)/shard_map/ppermute | solution.py:342
  73.8 6.0 %collective-permute-done.10 = bf16[512,384]{1,0:T(8,128)(2,1)S(1)} collective-permute-done((bf16[512,384]{1,0:T(8,128)(2,1)S(1)}, bf16[512,384]{1,0:T(8,128)(2,1)S(1)}, u32[]{:S(2)}, u32[]{:S(2)}) %collective-permute-start.10) | collective-permute-done | bytes 393248 | tf_op jit(solution)/shard_map/ppermute | solution.py:341
  79.7 0.7 slice.159
  80.4 0.7 slice.158
  81.1 3.2 %collective-permute-start.13 = (bf16[256,384]{1,0:T(8,128)(2,1)}, bf16[256,384]{1,0:T(8,128)(2,1)}, u32[]{:S(2)}, u32[]{:S(2)}) collective-permute-start(bf16[256,384]{1,0:T(8,128)(2,1)} %slice.158), channel_id=1, source_target_pairs={{0,1},{1,2},{2,3},{3,0},{4,5},{5,6},{6,7},{7,4},{8,9},{9,10},{10,1... | collective-permute-start | bytes 589832 | tf_op jit(solution)/shard_map/ppermute | solution.py:342
  84.4 1.8 %fusion.10 = f32[512,768]{1,0:T(8,128)S(1)} fusion(bf16[512,384]{1,0:T(8,128)(2,1)S(1)} %collective-permute-done.8, bf16[3072,768]{1,0:T(8,128)(2,1)} %all-gather.2.cloned.1.call-done, s32[]{:T(128)S(6)} %select_n.309), kind=kOutput, calls=%fused_computation.10 | convolution fusion | flops 301989888 | bytes 2555908 | tf_op jit(solution)/shard_map/dot_general | solution.py:351
  86.1 1.6 %fusion.6 = f32[512,768]{1,0:T(8,128)S(1)} fusion(bf16[512,384]{1,0:T(8,128)(2,1)S(1)} %collective-permute-done.10, bf16[3072,768]{1,0:T(8,128)(2,1)} %all-gather.2.cloned.1.call-done, s32[]{:T(128)S(6)} %select_n.312), kind=kOutput, calls=%fused_computation.6 | convolution fusion | flops 301989888 | bytes 2555908 | tf_op jit(solution)/shard_map/dot_general | solution.py:351
  87.8 0.6 fusion.12
  90.1 1.6 %fusion.4 = f32[512,768]{1,0:T(8,128)S(1)} fusion(bf16[3072,768]{1,0:T(8,128)(2,1)S(1)} %copy-done.8, s32[]{:T(128)S(6)} %select_n.314, bf16[256,384]{1,0:T(8,128)(2,1)} %collective-permute-done.12, bf16[256,384]{1,0:T(8,128)(2,1)} %collective-permute-done.11), kind=kOutput, calls=%fused_computation.4 | convolution fusion | flops 302776320 | bytes 2555908 | tf_op jit(solution)/shard_map/dot_general | solution.py:351
  91.7 2.6 %add_convert_fusion = bf16[512,768]{1,0:T(8,128)(2,1)} fusion(f32[512,768]{1,0:T(8,128)S(1)} %fusion.4, f32[512,768]{1,0:T(8,128)S(1)} %fusion.6, f32[512,768]{1,0:T(8,128)S(1)} %fusion.8, f32[512,768]{1,0:T(8,128)S(1)} %fusion.10, f32[512,768]{1,0:T(8,128)S(1)} %fusion.12, f32[512,768]{1,0:T(8,128)S(1)} %fusion.14, f32[512,768]{1,0:T(8,128)S(1)} %fusion.16, ...), kind=kOutput, calls=%fused_computation | convolution fusion | flops 306708480 | bytes 13565956 | tf_op jit(solution)/shard_map/dot_general | solution.py:351
  (59 shorter events, 2.9 us)
Async XLA Ops:
  6.5 77.8 %all-gather.2.cloned.1.call-start = ((), (), s32[]{:S(2)}) async-start(), calls=%async_computation | async-start | bytes 4866048 | tf_op jit(solution)/shard_map/all_gather | solution.py:280
  7.3 1.1 %copy-start.1 = (bf16[512,768]{1,0:T(8,128)(2,1)S(1)}, bf16[512,768]{1,0:T(8,128)(2,1)}, u32[]{:S(2)}) copy-start(bf16[512,768]{1,0:T(8,128)(2,1)} %u_ref.3) | copy-start | bytes 2359300
  8.4 0.9 copy-start.4
  9.3 0.9 copy-start.6
  19.5 1.7 %copy-start = (f32[16,2,32,768]{3,2,1,0:T(8,128)}, f32[16,2,32,768]{3,2,1,0:T(8,128)S(1)}, u32[]{:S(2)}) copy-start(f32[16,2,32,768]{3,2,1,0:T(8,128)S(1)} %get-tuple-element.12.part_ref) | copy-start | bytes 9437188
  21.2 5.5 %copy-start.10 = (f32[768]{0:T(1024)S(1)}, f32[768]{0:T(1024)}, u32[]{:S(2)}) copy-start(f32[768]{0:T(1024)} %param.10) | copy-start | bytes 9220
  21.2 5.5 %copy-start.2 = (bf16[512,768]{1,0:T(8,128)(2,1)S(1)}, bf16[512,768]{1,0:T(8,128)(2,1)}, u32[]{:S(2)}) copy-start(bf16[512,768]{1,0:T(8,128)(2,1)} %u_ref.3) | copy-start | bytes 2359300
  21.2 5.5 %copy-start.3 = (f32[2,32,768]{2,1,0:T(8,128)S(1)}, f32[2,32,768]{2,1,0:T(8,128)}, u32[]{:S(2)}) copy-start(f32[2,32,768]{2,1,0:T(8,128)} %c_ref.1) | copy-start | bytes 589828
  21.2 5.5 %copy-start.5 = (f32[32,768]{1,0:T(8,128)S(1)}, f32[32,768]{1,0:T(8,128)}, u32[]{:S(2)}) copy-start(f32[32,768]{1,0:T(8,128)} %r_ref.3) | copy-start | bytes 294916
  21.2 5.5 %copy-start.7 = (f32[32,768]{1,0:T(8,128)S(1)}, f32[32,768]{1,0:T(8,128)}, u32[]{:S(2)}) copy-start(f32[32,768]{1,0:T(8,128)} %f_ref.3) | copy-start | bytes 294916
  21.2 1.4 %collective-permute-start = (bf16[2,32,768]{2,1,0:T(8,128)(2,1)S(1)}, bf16[2,32,768]{2,1,0:T(8,128)(2,1)S(1)}, u32[]{:S(2)}, u32[]{:S(2)}) collective-permute-start(bf16[2,32,768]{2,1,0:T(8,128)(2,1)S(1)} %get-tuple-element.18), channel_id=1, source_target_pairs={{0,4},{4,0},{8,12},{12,8},{16,20},{20,16},{24,28},{28,24},{32,36},... | collective-permute-start | bytes 294920 | tf_op jit(solution)/shard_map/ppermute | solution.py:293
  22.7 13.3 %copy-start.9 = (f32[2,32,768]{2,1,0:T(8,128)S(1)}, f32[2,32,768]{2,1,0:T(8,128)}, u32[]{:S(2)}) copy-start(f32[2,32,768]{2,1,0:T(8,128)} %constant.100.clone.1) | copy-start | bytes 589828
  22.7 13.2 %collective-permute-start.2 = (bf16[2,32,768]{2,1,0:T(8,128)(2,1)S(1)}, bf16[2,32,768]{2,1,0:T(8,128)(2,1)S(1)}, u32[]{:S(2)}, u32[]{:S(2)}) collective-permute-start(bf16[2,32,768]{2,1,0:T(8,128)(2,1)S(1)} %fusion.25), channel_id=1, source_target_pairs={{0,16},{4,20},{8,24},{12,28},{16,0},{20,4},{24,8},{28,12},{32,48},... | collective-permute-start | bytes 294920 | tf_op jit(solution)/shard_map/ppermute | solution.py:311
  33.9 6.8 %collective-permute-start.3 = (bf16[2,32,768]{2,1,0:T(8,128)(2,1)S(1)}, bf16[2,32,768]{2,1,0:T(8,128)(2,1)S(1)}, u32[]{:S(2)}, u32[]{:S(2)}) collective-permute-start(bf16[2,32,768]{2,1,0:T(8,128)(2,1)S(1)} %fusion.25), channel_id=1, source_target_pairs={{0,24},{4,28},{8,0},{12,4},{16,8},{20,12},{24,16},{28,20},{32,56},... | collective-permute-start | bytes 294920 | tf_op jit(solution)/shard_map/ppermute | solution.py:311
  34.6 5.8 %collective-permute-start.1 = (bf16[2,32,768]{2,1,0:T(8,128)(2,1)S(1)}, bf16[2,32,768]{2,1,0:T(8,128)(2,1)S(1)}, u32[]{:S(2)}, u32[]{:S(2)}) collective-permute-start(bf16[2,32,768]{2,1,0:T(8,128)(2,1)S(1)} %fusion.25), channel_id=1, source_target_pairs={{0,8},{4,12},{8,16},{12,20},{16,24},{20,28},{24,0},{28,4},{32,40},... | collective-permute-start | bytes 294920 | tf_op jit(solution)/shard_map/ppermute | solution.py:311
  40.8 5.3 %collective-permute-start.6 = (bf16[2,32,768]{2,1,0:T(8,128)(2,1)S(1)}, bf16[2,32,768]{2,1,0:T(8,128)(2,1)S(1)}, u32[]{:S(2)}, u32[]{:S(2)}) collective-permute-start(bf16[2,32,768]{2,1,0:T(8,128)(2,1)S(1)} %fusion.30), channel_id=1, source_target_pairs={{0,96},{4,100},{8,104},{12,108},{16,112},{20,116},{24,120},{28,124... | collective-permute-start | bytes 294920 | tf_op jit(solution)/shard_map/ppermute | solution.py:321
  41.5 8.6 %collective-permute-start.5 = (bf16[2,32,768]{2,1,0:T(8,128)(2,1)S(1)}, bf16[2,32,768]{2,1,0:T(8,128)(2,1)S(1)}, u32[]{:S(2)}, u32[]{:S(2)}) collective-permute-start(bf16[2,32,768]{2,1,0:T(8,128)(2,1)S(1)} %fusion.30), channel_id=1, source_target_pairs={{0,64},{4,68},{8,72},{12,76},{16,80},{20,84},{24,88},{28,92},{32,9... | collective-permute-start | bytes 294920 | tf_op jit(solution)/shard_map/ppermute | solution.py:321
  44.2 7.6 %collective-permute-start.4 = (bf16[2,32,768]{2,1,0:T(8,128)(2,1)S(1)}, bf16[2,32,768]{2,1,0:T(8,128)(2,1)S(1)}, u32[]{:S(2)}, u32[]{:S(2)}) collective-permute-start(bf16[2,32,768]{2,1,0:T(8,128)(2,1)S(1)} %fusion.30), channel_id=1, source_target_pairs={{0,32},{4,36},{8,40},{12,44},{16,48},{20,52},{24,56},{28,60},{32,6... | collective-permute-start | bytes 294920 | tf_op jit(solution)/shard_map/ppermute | solution.py:321
  57.8 12.6 %collective-permute-start.9 = (bf16[512,384]{1,0:T(8,128)(2,1)S(1)}, bf16[512,384]{1,0:T(8,128)(2,1)S(1)}, u32[]{:S(2)}, u32[]{:S(2)}) collective-permute-start(bf16[512,384]{1,0:T(8,128)(2,1)S(1)} %shard_map.66), channel_id=1, source_target_pairs={{0,3},{1,0},{2,1},{3,2},{4,7},{5,4},{6,5},{7,6},{8,11},{9,8},{10,9... | collective-permute-start | bytes 1179656 | tf_op jit(solution)/shard_map/ppermute | solution.py:341
  58.5 11.9 %collective-permute-start.7 = (bf16[512,384]{1,0:T(8,128)(2,1)S(1)}, bf16[512,384]{1,0:T(8,128)(2,1)S(1)}, u32[]{:S(2)}, u32[]{:S(2)}) collective-permute-start(bf16[512,384]{1,0:T(8,128)(2,1)S(1)} %shard_map.66), channel_id=1, source_target_pairs={{0,1},{1,2},{2,3},{3,0},{4,5},{5,6},{6,7},{7,4},{8,9},{9,10},{10,1... | collective-permute-start | bytes 1179656 | tf_op jit(solution)/shard_map/ppermute | solution.py:340
  67.0 12.7 %collective-permute-start.10 = (bf16[512,384]{1,0:T(8,128)(2,1)S(1)}, bf16[512,384]{1,0:T(8,128)(2,1)S(1)}, u32[]{:S(2)}, u32[]{:S(2)}) collective-permute-start(bf16[512,384]{1,0:T(8,128)(2,1)S(1)} %shard_map.67), channel_id=1, source_target_pairs={{0,3},{1,0},{2,1},{3,2},{4,7},{5,4},{6,5},{7,6},{8,11},{9,8},{10,9... | collective-permute-start | bytes 1179656 | tf_op jit(solution)/shard_map/ppermute | solution.py:341
  67.1 13.3 %collective-permute-start.8 = (bf16[512,384]{1,0:T(8,128)(2,1)S(1)}, bf16[512,384]{1,0:T(8,128)(2,1)S(1)}, u32[]{:S(2)}, u32[]{:S(2)}) collective-permute-start(bf16[512,384]{1,0:T(8,128)(2,1)S(1)} %shard_map.67), channel_id=1, source_target_pairs={{0,1},{1,2},{2,3},{3,0},{4,5},{5,6},{6,7},{7,4},{8,9},{9,10},{10,1... | collective-permute-start | bytes 1179656 | tf_op jit(solution)/shard_map/ppermute | solution.py:340
  70.4 19.7 %collective-permute-start.12 = (bf16[256,384]{1,0:T(8,128)(2,1)S(1)}, bf16[256,384]{1,0:T(8,128)(2,1)}, u32[]{:S(2)}, u32[]{:S(2)}) collective-permute-start(bf16[256,384]{1,0:T(8,128)(2,1)S(1)} %slice.157), channel_id=1, source_target_pairs={{0,3},{1,0},{2,1},{3,2},{4,7},{5,4},{6,5},{7,6},{8,11},{9,8},{10,9... | collective-permute-start | bytes 589832 | tf_op jit(solution)/shard_map/ppermute | solution.py:343
  70.5 19.6 %collective-permute-start.11 = (bf16[256,384]{1,0:T(8,128)(2,1)S(1)}, bf16[256,384]{1,0:T(8,128)(2,1)}, u32[]{:S(2)}, u32[]{:S(2)}) collective-permute-start(bf16[256,384]{1,0:T(8,128)(2,1)S(1)} %slice.156), channel_id=1, source_target_pairs={{0,1},{1,2},{2,3},{3,0},{4,5},{5,6},{6,7},{7,4},{8,9},{9,10},{10,1... | collective-permute-start | bytes 589832 | tf_op jit(solution)/shard_map/ppermute | solution.py:342
  80.4 11.3 %collective-permute-start.14 = (bf16[256,384]{1,0:T(8,128)(2,1)}, bf16[256,384]{1,0:T(8,128)(2,1)}, u32[]{:S(2)}, u32[]{:S(2)}) collective-permute-start(bf16[256,384]{1,0:T(8,128)(2,1)} %slice.159), channel_id=1, source_target_pairs={{0,3},{1,0},{2,1},{3,2},{4,7},{5,4},{6,5},{7,6},{8,11},{9,8},{10,9... | collective-permute-start | bytes 589832 | tf_op jit(solution)/shard_map/ppermute | solution.py:343
  81.1 10.6 %collective-permute-start.13 = (bf16[256,384]{1,0:T(8,128)(2,1)}, bf16[256,384]{1,0:T(8,128)(2,1)}, u32[]{:S(2)}, u32[]{:S(2)}) collective-permute-start(bf16[256,384]{1,0:T(8,128)(2,1)} %slice.158), channel_id=1, source_target_pairs={{0,1},{1,2},{2,3},{3,0},{4,5},{5,6},{6,7},{7,4},{8,9},{9,10},{10,1... | collective-permute-start | bytes 589832 | tf_op jit(solution)/shard_map/ppermute | solution.py:342
  84.4 3.4 %copy-start.8 = (bf16[3072,768]{1,0:T(8,128)(2,1)S(1)}, bf16[3072,768]{1,0:T(8,128)(2,1)}, u32[]{:S(2)}) copy-start(bf16[3072,768]{1,0:T(8,128)(2,1)} %all-gather.2.cloned.1.call-done) | copy-start | bytes 14155780
Sparse Core Ops, SparseCore 0:
  9.6 51.5 all-gather.1

commit v2 on v1

--- a/solution.py
+++ b/solution.py
@@ -23,7 +23,7 @@
     return size * jnp.cos(angle), size * jnp.sin(angle)
 
 
-def ends_kernel(u_ref, r_ref, f_ref, part_ref, end_ref, send_ref, step_ref, whole_ref, uf, table):
+def ends_kernel(u_ref, r_ref, f_ref, part_ref, end_ref, send_ref, step_ref, power_ref, uf, table):
     uf[...] = u_ref[...].astype(f32)
     lr, li = decay(r_ref, f_ref)
     powers = [(jnp.ones_like(lr), jnp.zeros_like(lr)), (lr, li)]
@@ -41,8 +41,10 @@
     while count < u_ref.shape[0]:
         wr, wi = cmul(wr, wi, wr, wi)
         count *= 2
-    whole_ref[0] = wr
-    whole_ref[1] = wi
+    for k in range(power_ref.shape[0]):
+        power_ref[k, 0] = wr
+        power_ref[k, 1] = wi
+        wr, wi = cmul(wr, wi, wr, wi)
 
     def group(g, end):
         er, ei = end
@@ -103,7 +105,7 @@
         return tuple(out)
 
     zero = jnp.zeros((8, LANES), f32)
-    sums = lax.fori_loop(0, modes, mode, (zero,) * (BLK // 8), unroll=2)
+    sums = lax.fori_loop(0, modes, mode, (zero,) * (BLK // 8), unroll=8)
     taps[0:1] = jnp.sum(cr, axis=0, keepdims=True) + skip_ref[...]
     for i in range(BLK // 8):
         taps[8 * i + 1 : 8 * i + 9] = sums[i]
@@ -127,13 +129,12 @@
     lax.fori_loop(0, blocks // GROUP, group, 0)
 
 
-def finish_kernel(part_ref, step_ref, coef_ref, base_ref, own_ref, w_ref, q1_ref, q2_ref, q3_ref, act_ref, held):
+def finish_kernel(part_ref, step_ref, coef_ref, base_ref, own_ref, w_ref, q_ref, act_ref, held):
     hr = own_ref[0]
     hi = own_ref[1]
-    for k, q in enumerate((q1_ref, q2_ref, q3_ref)):
-        ar, ai = cmul(w_ref[k, 0], w_ref[k, 1], q[0].astype(f32), q[1].astype(f32))
-        hr = hr + ar
-        hi = hi + ai
+    ar, ai = cmul(w_ref[0], w_ref[1], q_ref[0].astype(f32), q_ref[1].astype(f32))
+    hr = hr + ar
+    hi = hi + ai
     sr = step_ref[0]
     si = step_ref[1]
     blocks = part_ref.shape[0]
@@ -170,7 +171,7 @@
     lax.fori_loop(0, blocks // many, group, 0)
 
 
-def params(limit=48):
+def params(limit=60):
     return pltpu.CompilerParams(vmem_limit_bytes=limit << 20)
 
 
@@ -192,14 +193,14 @@
             pair,
             pair,
             pair,
-            pair,
+            pl.BlockSpec((4, 2, modes, LANES), lambda i: (0, 0, 0, i)),
         ],
         out_shape=[
             jax.ShapeDtypeStruct((blocks, 2, modes, channels), f32),
             jax.ShapeDtypeStruct((2, modes, channels), f32),
             jax.ShapeDtypeStruct((2, modes, channels), bf16),
             jax.ShapeDtypeStruct((2, modes, channels), f32),
-            jax.ShapeDtypeStruct((2, modes, channels), f32),
+            jax.ShapeDtypeStruct((4, 2, modes, channels), f32),
         ],
         scratch_shapes=[
             pltpu.VMEM((tokens, LANES), f32),
@@ -210,39 +211,41 @@
     )(signal, rates, freqs)
 
 
-def inner(signal, rates, freqs, coeffs, skip):
-    tokens, channels = signal.shape
+def inner(first, count, signal, rates, freqs, coeffs, skip):
+    tokens = signal.shape[0]
     modes = rates.shape[0]
     blocks = tokens // BLK
     return pl.pallas_call(
         inner_kernel,
-        grid=(channels // LANES,),
+        grid=(count,),
         in_specs=[
-            pl.BlockSpec((tokens, LANES), lambda i: (0, i)),
-            pl.BlockSpec((modes, LANES), lambda i: (0, i)),
-            pl.BlockSpec((modes, LANES), lambda i: (0, i)),
-            pl.BlockSpec((2, modes, LANES), lambda i: (0, 0, i)),
-            pl.BlockSpec((1, LANES), lambda i: (0, i)),
+            pl.BlockSpec((tokens, LANES), lambda i: (0, i + first)),
+            pl.BlockSpec((modes, LANES), lambda i: (0, i + first)),
+            pl.BlockSpec((modes, LANES), lambda i: (0, i + first)),
+            pl.BlockSpec((2, modes, LANES), lambda i: (0, 0, i + first)),
+            pl.BlockSpec((1, LANES), lambda i: (0, i + first)),
         ],
         out_specs=[
             pl.BlockSpec((modes, 2, BLK, LANES), lambda i: (0, 0, 0, i)),
             pl.BlockSpec((tokens, LANES), lambda i: (0, i)),
         ],
         out_shape=[
-            jax.ShapeDtypeStruct((modes, 2, BLK, channels), f32),
-            jax.ShapeDtypeStruct((tokens, channels), f32),
+            jax.ShapeDtypeStruct((modes, 2, BLK, count * LANES), f32),
+            jax.ShapeDtypeStruct((tokens, count * LANES), f32),
         ],
         scratch_shapes=[
             pltpu.VMEM((blocks, BLK + 8, LANES), f32),
             pltpu.VMEM((10, modes, LANES), f32),
             pltpu.VMEM((BLK + 8, LANES), f32),
         ],
-        compiler_params=params(),
-        cost_estimate=pl.CostEstimate(flops=5 * 10**8, bytes_accessed=8 * 10**6, transcendentals=0),
-    )(signal, rates, freqs, coeffs, skip.reshape(1, channels))
-
-
-def finish(first, count, part, step, coef, base, own, weights, arrived):
+        compiler_params=params(14),
+        cost_estimate=pl.CostEstimate(
+            flops=10**8 * count, bytes_accessed=2 * 10**6 * count, transcendentals=0
+        ),
+    )(signal, rates, freqs, coeffs, skip)
+
+
+def finish(first, count, part, step, coef, base, own, weight, arrived):
     blocks, _, modes, _ = part.shape
     tokens = base.shape[0]
     pair = pl.BlockSpec((2, modes, LANES), lambda i: (0, 0, i + first))
@@ -252,10 +255,8 @@
         in_specs=[
             pl.BlockSpec((blocks, 2, modes, LANES), lambda i: (0, 0, 0, i + first)),
             pair,
-            pl.BlockSpec((modes, 2, BLK, LANES), lambda i: (0, 0, 0, i + first)),
-            pl.BlockSpec((tokens, LANES), lambda i: (0, i + first)),
-            pair,
-            pl.BlockSpec((3, 2, modes, LANES), lambda i: (0, 0, 0, i + first)),
+            pl.BlockSpec((modes, 2, BLK, LANES), lambda i: (0, 0, 0, i)),
+            pl.BlockSpec((tokens, LANES), lambda i: (0, i)),
             pair,
             pair,
             pair,
@@ -263,11 +264,50 @@
         out_specs=pl.BlockSpec((tokens, LANES), lambda i: (0, i)),
         out_shape=jax.ShapeDtypeStruct((tokens, count * LANES), bf16),
         scratch_shapes=[pltpu.VMEM((blocks, 2, modes, LANES), f32)],
-        compiler_params=params(),
+        compiler_params=params(14),
         cost_estimate=pl.CostEstimate(
             flops=10**9 // 6 * count, bytes_accessed=2 * 10**6 * count, transcendentals=0
         ),
-    )(part, step, coef, base, own, weights, *arrived)
+    )(part, step, coef, base, own, weight, arrived)
+
+
+def product_kernel(count, last, place_ref, *refs):
+    acts = refs[:count]
+    wide_ref = refs[count]
+    more = refs[count + 1 : -1]
+    out_ref = refs[-1]
+    tile = out_ref.shape[1]
+    depth = wide_ref.shape[0] // 4
+    span = pl.ds(pl.multiple_of(pl.program_id(0) * tile, tile), tile)
+    total = None
+    for n, act in enumerate(acts):
+        width = act.shape[1]
+        start = place_ref[2 * n] * depth + place_ref[2 * n + 1] * width
+        rows = pl.ds(pl.multiple_of(start, LANES), width)
+        term = jnp.dot(act[...], wide_ref[rows, span], preferred_element_type=f32)
+        total = term if total is None else total + term
+    if last:
+        total = total + more[0][:, span] + more[1][:, span].astype(f32)
+    out_ref[...] = total.astype(out_ref.dtype)
+
+
+def product(place, acts, wide, *more):
+    tokens = acts[0].shape[0]
+    channels = wide.shape[1]
+    tile = 256
+    inside = pl.BlockSpec(memory_space=pltpu.VMEM)
+    last = bool(more)
+    return pl.pallas_call(
+        lambda *refs: product_kernel(len(acts), last, *refs),
+        grid=(channels // tile,),
+        in_specs=[pl.BlockSpec(memory_space=pltpu.SMEM)] + [inside] * (len(acts) + 1 + len(more)),
+        out_specs=pl.BlockSpec((tokens, tile), lambda n: (0, n)),
+        out_shape=jax.ShapeDtypeStruct((tokens, channels), bf16 if last else f32),
+        compiler_params=params(12),
+        cost_estimate=pl.CostEstimate(
+            flops=4 * 10**8 * len(acts), bytes_accessed=10**6 * len(acts), transcendentals=0
+        ),
+    )(place, *acts, wide, *more)
 
 
 def times(a, b):
@@ -276,80 +316,61 @@
     return jnp.stack([ar * br - ai * bi, ar * bi + ai * br])
 
 
+def partners(step):
+    return [(i, i ^ step) for i in range(32)]
+
+
+Y_STEP = [[(i, (i + k) % 4) for i in range(4)] for k in range(4)]
+
+
+def after(value, *others):
+    return lax.optimization_barrier((value, *others))[0]
+
+
 def local(signal, rates, freqs, coeffs, skip, weight):
+    index = lax.axis_index("seq")
+    y = lax.axis_index("chan")
+    skip = skip.reshape(1, -1)
     wide = lax.all_gather(weight, "seq", axis=0, tiled=True)
-    part, end, send, step, whole = ends(signal, rates, freqs)
-
-    index = lax.axis_index("seq")
-    x, z, c = index // 8, index // 2 % 4, index % 2
-    core = [(i, i ^ 1) for i in range(32)]
-
-    def along_z(k):
-        return [(i, i // 8 * 8 + (i // 2 + k) % 4 * 2 + i % 2) for i in range(32)]
-
-    def along_x(k):
-        return [(i, (i + 8 * k) % 32) for i in range(32)]
-
-    other = lax.ppermute(send, "seq", core).astype(f32)
-    lower = jnp.where(c == 0, end, other)
-    upper = jnp.where(c == 0, other, end)
-    chip = (times(whole, lower) + upper).astype(bf16)
-
-    unit = jnp.stack([jnp.ones_like(rates), jnp.zeros_like(rates)])
-    p1 = times(whole, whole)
-    p2 = times(p1, p1)
-    p3 = times(p2, p1)
-    p4 = times(p2, p2)
-    p8 = times(p4, p4)
-    chips = [unit, p1, p2, p3]
-
-    def pick(k):
-        return jnp.where(k == 0, unit, jnp.where(k == 1, p1, jnp.where(k == 2, p2, p3)))
-
-    mine = jnp.where(c == 0, unit, whole)
-
-    from_z = [lax.ppermute(chip, "seq", along_z(k)) for k in (1, 2, 3)]
-    line = times(pick(3 - z), chip)
-    for k in (1, 2, 3):
-        line = line + times(pick(3 - (z - k) % 4), from_z[k - 1])
-    line = line.astype(bf16)
+    part, end, send, step, powers = ends(signal, rates, freqs)
+
+    mine = end
+    scale = jnp.stack([jnp.ones_like(rates), jnp.zeros_like(rates)])
     own = jnp.zeros_like(end)
-    for k in (1, 2, 3):
-        own = own + jnp.where(z >= k, times(chips[k - 1], from_z[k - 1]), 0.0)
-    own = times(mine, own) + jnp.where(c == 1, lower, 0.0)
-
-    from_x = [lax.ppermute(line, "seq", along_x(k)) for k in (1, 2, 3)]
-    here = times(mine, pick(z))
-    weights = jnp.stack(
-        [
-            jnp.where(x >= k, times(here, far), 0.0)
-            for k, far in ((1, unit), (2, p4), (3, p8))
-        ]
-    )
-    coef, base = inner(signal, rates, freqs, coeffs, skip)
-
-    slabs = 2
-    count = signal.shape[1] // LANES // slabs
-    ring = lambda k: [(i, (i + k) % 4) for i in range(4)]
-    half = signal.shape[0] // 2
-    y = lax.axis_index("chan")
-    width = count * LANES
-    pieces = []
-    for s in range(slabs):
-        act = finish(s * count, count, part, step, coef, base, own, weights, from_x)
-        up = lax.ppermute(act, "chan", ring(1))
-        down = lax.ppermute(act, "chan", ring(3))
-        far_up = lax.ppermute(up[:half], "chan", ring(1))
-        far_down = lax.ppermute(down[half:], "chan", ring(3))
-        pieces.append((act, up, down, jnp.concatenate([far_up, far_down])))
-    total = signal.astype(f32)
-    for k, off in enumerate((0, 3, 1, 2)):
-        for s in range(slabs):
-            rows = lax.dynamic_slice_in_dim(
-                wide, (y + off) % 4 * signal.shape[1] + s * width, width, 0
-            )
-            total = total + jnp.dot(pieces[s][k], rows, preferred_element_type=f32)
-    return total.astype(bf16)
+    inners = []
+    for k in range(5):
+        upper = (index >> k) % 2 == 1
+        arrived = lax.ppermute(send, "seq", partners(1 << k))
+        if k in (2, 3):
+            s = k - 2
+            inners.append(inner(3 * s, 3, after(signal, send), rates, freqs, coeffs, skip))
+        if k == 4:
+            scale = jnp.where(upper, scale, 0.0)
+            break
+        other = arrived.astype(f32)
+        low = jnp.where(upper, other, mine)
+        high = jnp.where(upper, mine, other)
+        own = own + jnp.where(upper, times(scale, arrived), 0.0)
+        scale = jnp.where(upper, times(scale, powers[k]), scale)
+        mine = times(powers[k], low) + high
+        send = mine.astype(bf16)
+
+    acts, ups, downs, fars = [], [], [], []
+    for s in range(2):
+        act = finish(3 * s, 3, part, step, *inners[s], own, scale, arrived)
+        up = lax.ppermute(act, "chan", Y_STEP[1])
+        down = lax.ppermute(act, "chan", Y_STEP[3])
+        fars.append(lax.ppermute(down if s else up, "chan", Y_STEP[3 if s else 1]))
+        acts.append(act)
+        ups.append(up)
+        downs.append(down)
+    mine, below, above, across = y, (y + 3) % 4, (y + 1) % 4, (y + 2) % 4
+    zero = jnp.zeros_like(y)
+    one = zero + 1
+    first = jnp.stack([mine, zero, mine, one, below, zero, above, zero]).astype(jnp.int32)
+    second = jnp.stack([below, one, above, one, across, zero, across, one]).astype(jnp.int32)
+    total = product(first, [*acts, ups[0], downs[0]], wide)
+    return product(second, [ups[1], downs[1], *fars], wide, total, signal)
 
 
 def solution(mesh):

time: 103 us -> 96.4 us (0.936); the launches traced: 101 us -> 96.1 us
  matrix products: 9.95 us -> 0 us
  waiting for transfers between devices: 19.7 us -> 28.7 us
  starting transfers between devices: 22.6 us -> 14.6 us
  Pallas kernels: 28.3 us -> 33 us
  local copies, waits for them, and re-layouts: 6.1 us -> 2.55 us
  other arithmetic: 0.82 us -> 3.63 us
    dot_general x8 -> x0, matrix products: 9.95 us -> none  [local(): total = total + jnp.dot(pieces[s][k], rows, preferred_element_type=f32)]
    ppermute x15 -> x11, waiting for transfers between devices: 19 us -> 28 us  [the longest x2 16.2 us: local(): down = lax.ppermute(act, 'chan', Y_STEP[3])]
    ppermute x15 -> x11, starting transfers between devices: 22.6 us -> 14.6 us  [the longest x5 8.24 us: local(): arrived = lax.ppermute(send, 'seq', partners(1 << k))]
    pallas_call x1 -> x4, Pallas kernels: 7.14 us -> 12.4 us  [the longest x2 6.76 us: product(): pl.pallas_call(lambda *refs: product_kernel(len(acts), last, *refs), grid...]
    unnamed x22, local copies, waits for them, and re-layouts: 4.67 us -> 2.38 us
    pallas_call x2, Pallas kernels: 11.9 us -> 9.74 us  [finish(): pl.pallas_call(finish_kernel, grid=(count,), in_specs=[pl.BlockSpec((bloc...]
    sub x5 -> x8, other arithmetic: 0.24 us -> 2.21 us  [times(): return jnp.stack([ar * br - ai * bi, ar * bi + ai * br])]
    pallas_call x1, Pallas kernels: 9.27 us -> 10.8 us  [ends(): pl.pallas_call(ends_kernel, grid=(channels // LANES,), in_specs=[pl.Block...]
  transfers between devices with their start and end apart: 16 -> 12, of which waited for: 6 -> 7; matrix products, arithmetic and copies ran while one was open for 9% -> 4% of each run, Pallas kernels for 28% -> 30%
where the time goes in v2:
time: 96.4 us; the launch traced here: 96.1 us
  Pallas kernels  33 us (34%)
  waiting for transfers between devices  28.7 us (30%)
  starting transfers between devices  14.6 us (15%)
  between operations  13.7 us (14%)
  other arithmetic  3.63 us (4%)
  local copies, waits for them, and re-layouts  2.55 us (3%)
    ppermute x2, waiting for transfers between devices, local(): down = lax.ppermute(act, 'chan', Y_STEP[3])  16.2 us
    ppermute x5, waiting for transfers between devices, local(): arrived = lax.ppermute(send, 'seq', partners(1 << k))  11.8 us
    pallas_call x1, Pallas kernels, ends(): pl.pallas_call(ends_kernel, grid=(channels // LANES,), in_specs=[pl.Block...  10.8 us
    pallas_call x2, Pallas kernels, finish(): pl.pallas_call(finish_kernel, grid=(count,), in_specs=[pl.BlockSpec((bloc...  9.74 us
    ppermute x5, starting transfers between devices, local(): arrived = lax.ppermute(send, 'seq', partners(1 << k))  8.24 us
    pallas_call x2, Pallas kernels, product(): pl.pallas_call(lambda *refs: product_kernel(len(acts), last, *refs), grid...  6.76 us
    pallas_call x2, Pallas kernels, inner(): pl.pallas_call(inner_kernel, grid=(count,), in_specs=[pl.BlockSpec((token...  5.64 us
    ppermute x2, starting transfers between devices, local(): up = lax.ppermute(act, 'chan', Y_STEP[1])  3.2 us
  transfers between devices with their start and end apart: 12, of which 7 were waited for; matrix products, arithmetic and copies ran while one was open for 4% of the time, Pallas kernels for 30%

profile of v2, /device:TPU:28, one launch (start us, length us, event | category | flops | bytes accessed | tf_op | source)
XLA Modules:
  0.0 96.1 jit_solution(9312991101676690816)
XLA Ops:
  6.5 0.7 all-gather.2.cloned.1.call-update
  7.3 10.8 %shard_map.64 = (f32[16,2,32,768]{3,2,1,0:T(8,128)}, f32[2,32,768]{2,1,0:T(8,128)}, bf16[2,32,768]{2,1,0:T(8,128)(2,1)}, f32[2,32,768]{2,1,0:T(8,128)}, f32[4,2,32,768]{3,2,1,0:T(8,128)}) custom-call(bf16[512,768]{1,0:T(8,128)(2,1)} %refs_7_.1, f32[32,768]{1,0:T(8,128)} %r_ref.5, f32[32,768]{1,0:T(8,128)} %f_ref.5), custom_call_target="tpu_custom_call" | custom-call | flops 1000000000 | bytes 6000000 | tf_op jit(solution)/shard_map/pallas_call | solution.py:183
  18.1 0.1 collective-permute-start
  18.2 1.5 %collective-permute-done = bf16[2,32,768]{2,1,0:T(8,128)(2,1)S(1)} collective-permute-done((bf16[2,32,768]{2,1,0:T(8,128)(2,1)}, bf16[2,32,768]{2,1,0:T(8,128)(2,1)S(1)}, u32[]{:S(2)}, u32[]{:S(2)}) %collective-permute-start) | collective-permute-done | bytes 98336 | tf_op jit(solution)/shard_map/ppermute | solution.py:343
  19.7 0.9 convert_select_fusion.7
  20.7 1.0 %fusion.27 = (f32[1,32,768]{2,1,0:T(8,128)S(1)}, f32[1,32,768]{2,1,0:T(8,128)S(1)}) fusion(f32[2,32,768]{2,1,0:T(8,128)S(1)} %convert_select_fusion.7, f32[4,2,32,768]{3,2,1,0:T(8,128)} %get-tuple-element.18), kind=kLoop, calls=%fused_computation.79 | loop fusion | flops 147456 | bytes 589824 | tf_op jit(solution)/shard_map/sub | solution.py:316
  21.7 2.0 %collective-permute-start.1 = (bf16[2,32,768]{2,1,0:T(8,128)(2,1)S(1)}, bf16[2,32,768]{2,1,0:T(8,128)(2,1)S(1)}, u32[]{:S(2)}, u32[]{:S(2)}) collective-permute-start(bf16[2,32,768]{2,1,0:T(8,128)(2,1)S(1)} %get-tuple-element.31), channel_id=1, source_target_pairs={{0,8},{4,12},{8,0},{12,4},{16,24},{20,28},{24,16},{28,20},{32,40},... | collective-permute-start | bytes 294920 | tf_op jit(solution)/shard_map/ppermute | solution.py:343
  23.7 3.6 %collective-permute-done.1 = bf16[2,32,768]{2,1,0:T(8,128)(2,1)S(1)} collective-permute-done((bf16[2,32,768]{2,1,0:T(8,128)(2,1)S(1)}, bf16[2,32,768]{2,1,0:T(8,128)(2,1)S(1)}, u32[]{:S(2)}, u32[]{:S(2)}) %collective-permute-start.1) | collective-permute-done | bytes 98336 | tf_op jit(solution)/shard_map/ppermute | solution.py:343
  27.4 1.0 %fusion.23 = (f32[1,32,768]{2,1,0:T(8,128)S(1)}, f32[1,32,768]{2,1,0:T(8,128)S(1)}) fusion(f32[2,32,768]{2,1,0:T(8,128)S(1)} %convert_select_fusion.5, f32[4,2,32,768]{3,2,1,0:T(8,128)} %get-tuple-element.18), kind=kLoop, calls=%fused_computation.71 | loop fusion | flops 147456 | bytes 589824 | tf_op jit(solution)/shard_map/sub | solution.py:316
  28.4 3.8 %collective-permute-start.2 = (bf16[2,32,768]{2,1,0:T(8,128)(2,1)S(1)}, bf16[2,32,768]{2,1,0:T(8,128)(2,1)S(1)}, u32[]{:S(2)}, u32[]{:S(2)}) collective-permute-start(bf16[2,32,768]{2,1,0:T(8,128)(2,1)S(1)} %get-tuple-element.29), channel_id=1, source_target_pairs={{0,16},{4,20},{8,24},{12,28},{16,0},{20,4},{24,8},{28,12},{32,48},... | collective-permute-start | bytes 294920 | tf_op jit(solution)/shard_map/ppermute | solution.py:343
  32.3 2.8 %shard_map.67 = (f32[32,2,32,384]{3,2,1,0:T(8,128)S(1)}, f32[512,384]{1,0:T(8,128)S(1)}) custom-call(bf16[512,768]{1,0:T(8,128)(2,1)S(1)} %copy-done.3, f32[32,768]{1,0:T(8,128)S(1)} %copy-done.6, f32[32,768]{1,0:T(8,128)S(1)} %copy-done.7, f32[2,32,768]{2,1,0:T(8,128)S(1)} %copy-done.4, f32[1,768]{1,0:T(1,128)S(1)} %reshape.87.skip_ref), custom_call_target="tpu_custom_call" | custom-call | flops 300000000 | bytes 6000000 | tf_op jit(solution)/shard_map/pallas_call | solution.py:218
  35.1 0.1 collective-permute-done.2
  35.3 1.5 %collective-permute-start.3 = (bf16[2,32,768]{2,1,0:T(8,128)(2,1)S(1)}, bf16[2,32,768]{2,1,0:T(8,128)(2,1)S(1)}, u32[]{:S(2)}, u32[]{:S(2)}) collective-permute-start(bf16[2,32,768]{2,1,0:T(8,128)(2,1)S(1)} %get-tuple-element.27), channel_id=1, source_target_pairs={{0,32},{4,36},{8,40},{12,44},{16,48},{20,52},{24,56},{28,60},{32,0... | collective-permute-start | bytes 294920 | tf_op jit(solution)/shard_map/ppermute | solution.py:343
  36.9 2.8 %shard_map.65 = (f32[32,2,32,384]{3,2,1,0:T(8,128)S(1)}, f32[512,384]{1,0:T(8,128)S(1)}) custom-call(bf16[512,768]{1,0:T(8,128)(2,1)S(1)} %copy-done.3, f32[32,768]{1,0:T(8,128)S(1)} %copy-done.6, f32[32,768]{1,0:T(8,128)S(1)} %copy-done.7, f32[2,32,768]{2,1,0:T(8,128)S(1)} %copy-done.4, f32[1,768]{1,0:T(1,128)S(1)} %reshape.87.skip_ref), custom_call_target="tpu_custom_call" | custom-call | flops 300000000 | bytes 6000000 | tf_op jit(solution)/shard_map/pallas_call | solution.py:218
  39.7 0.3 collective-permute-done.3
  40.1 0.8 collective-permute-start.4
  41.2 0.1 fusion.7
  41.3 6.4 %collective-permute-done.4.q_ref = bf16[2,32,768]{2,1,0:T(8,128)(2,1)S(1)} collective-permute-done((bf16[2,32,768]{2,1,0:T(8,128)(2,1)S(1)}, bf16[2,32,768]{2,1,0:T(8,128)(2,1)S(1)}, u32[]{:S(2)}, u32[]{:S(2)}) %collective-permute-start.4) | collective-permute-done | bytes 98336 | tf_op jit(solution)/shard_map/ppermute | solution.py:343
  47.7 4.9 %shard_map.68.refs_1_ = bf16[512,384]{1,0:T(8,128)(2,1)S(1)} custom-call(f32[16,2,32,768]{3,2,1,0:T(8,128)S(1)} %copy-done.2, f32[2,32,768]{2,1,0:T(8,128)S(1)} %copy-done.5, f32[32,2,32,384]{3,2,1,0:T(8,128)S(1)} %get-tuple-element.25.coef_ref, f32[512,384]{1,0:T(8,128)S(1)} %get-tuple-element.26.base_ref, f32[2,32,768]{2,1,0:T(8,128)S(1)} %get-tuple-element.63.own_ref, ...), custom_call_target="tpu_custom_call" | custom-call | flops 500000000 | bytes 6000000 | tf_op jit(solution)/shard_map/pallas_call | solution.py:252
  52.6 1.0 %collective-permute-start.7 = (bf16[512,384]{1,0:T(8,128)(2,1)S(1)}, bf16[512,384]{1,0:T(8,128)(2,1)S(1)}, u32[]{:S(2)}, u32[]{:S(2)}) collective-permute-start(bf16[512,384]{1,0:T(8,128)(2,1)S(1)} %shard_map.68.refs_1_), channel_id=1, source_target_pairs={{0,1},{1,2},{2,3},{3,0},{4,5},{5,6},{6,7},{7,4},{8,9},{9,10},{10,1... | collective-permute-start | bytes 1179656 | tf_op jit(solution)/shard_map/ppermute | solution.py:361
  53.6 4.9 %shard_map.66.refs_2_ = bf16[512,384]{1,0:T(8,128)(2,1)S(1)} custom-call(f32[16,2,32,768]{3,2,1,0:T(8,128)S(1)} %copy-done.2, f32[2,32,768]{2,1,0:T(8,128)S(1)} %copy-done.5, f32[32,2,32,384]{3,2,1,0:T(8,128)S(1)} %get-tuple-element.22.coef_ref, f32[512,384]{1,0:T(8,128)S(1)} %get-tuple-element.23.base_ref, f32[2,32,768]{2,1,0:T(8,128)S(1)} %get-tuple-element.63.own_ref, ...), custom_call_target="tpu_custom_call" | custom-call | flops 500000000 | bytes 6000000 | tf_op jit(solution)/shard_map/pallas_call | solution.py:252
  58.5 1.2 %collective-permute-start.6 = (bf16[512,384]{1,0:T(8,128)(2,1)S(1)}, bf16[512,384]{1,0:T(8,128)(2,1)S(1)}, u32[]{:S(2)}, u32[]{:S(2)}) collective-permute-start(bf16[512,384]{1,0:T(8,128)(2,1)S(1)} %shard_map.66.refs_2_), channel_id=1, source_target_pairs={{0,3},{1,0},{2,1},{3,2},{4,7},{5,4},{6,5},{7,6},{8,11},{9,8},{10,9... | collective-permute-start | bytes 1179656 | tf_op jit(solution)/shard_map/ppermute | solution.py:362
  59.6 1.0 %collective-permute-start.10 = (bf16[512,384]{1,0:T(8,128)(2,1)S(1)}, bf16[512,384]{1,0:T(8,128)(2,1)S(1)}, u32[]{:S(2)}, u32[]{:S(2)}) collective-permute-start(bf16[512,384]{1,0:T(8,128)(2,1)S(1)} %shard_map.68.refs_1_), channel_id=1, source_target_pairs={{0,3},{1,0},{2,1},{3,2},{4,7},{5,4},{6,5},{7,6},{8,11},{9,8},{10,9... | collective-permute-start | bytes 1179656 | tf_op jit(solution)/shard_map/ppermute | solution.py:362
  60.7 2.2 %collective-permute-start.5 = (bf16[512,384]{1,0:T(8,128)(2,1)S(1)}, bf16[512,384]{1,0:T(8,128)(2,1)S(1)}, u32[]{:S(2)}, u32[]{:S(2)}) collective-permute-start(bf16[512,384]{1,0:T(8,128)(2,1)S(1)} %shard_map.66.refs_2_), channel_id=1, source_target_pairs={{0,1},{1,2},{2,3},{3,0},{4,5},{5,6},{6,7},{7,4},{8,9},{9,10},{10,1... | collective-permute-start | bytes 1179656 | tf_op jit(solution)/shard_map/ppermute | solution.py:361
  62.9 0.9 collective-permute-start.8
  63.8 8.0 %collective-permute-done.6.refs_2_ = bf16[512,384]{1,0:T(8,128)(2,1)S(1)} collective-permute-done((bf16[512,384]{1,0:T(8,128)(2,1)S(1)}, bf16[512,384]{1,0:T(8,128)(2,1)S(1)}, u32[]{:S(2)}, u32[]{:S(2)}) %collective-permute-start.6) | collective-permute-done | bytes 393248 | tf_op jit(solution)/shard_map/ppermute | solution.py:362
  71.8 0.1 stack.99.refs_0_
  71.9 0.1 stack.39.refs_0_
  72.0 8.2 %collective-permute-done.10.refs_4_ = bf16[512,384]{1,0:T(8,128)(2,1)S(1)} collective-permute-done((bf16[512,384]{1,0:T(8,128)(2,1)S(1)}, bf16[512,384]{1,0:T(8,128)(2,1)S(1)}, u32[]{:S(2)}, u32[]{:S(2)}) %collective-permute-start.10) | collective-permute-done | bytes 393248 | tf_op jit(solution)/shard_map/ppermute | solution.py:362
  80.1 2.3 %copy-done = bf16[3072,768]{1,0:T(8,128)(2,1)S(1)} copy-done((bf16[3072,768]{1,0:T(8,128)(2,1)S(1)}, bf16[3072,768]{1,0:T(8,128)(2,1)}, u32[]{:S(2)}) %copy-start) | copy-done | bytes 4718616
  82.5 2.8 %shard_map.69.refs_6_ = f32[512,768]{1,0:T(8,128)S(1)} custom-call(s32[8]{0:T(128)S(1)} %stack.99.refs_0_, bf16[512,384]{1,0:T(8,128)(2,1)S(1)} %shard_map.68.refs_1_, bf16[512,384]{1,0:T(8,128)(2,1)S(1)} %shard_map.66.refs_2_, bf16[512,384]{1,0:T(8,128)(2,1)S(1)} %collective-permute-done.7.refs_3_, bf16[512,384]{1,0:T(8,128)(2,1)S(1)} %collective-permute-done.10.refs_4_, ...), custom_call_target="tpu_custom_call" | custom-call | flops 1600000000 | bytes 4000000 | tf_op jit(solution)/shard_map/pallas_call | solution.py:300
  85.3 4.0 %shard_map.70 = bf16[512,768]{1,0:T(8,128)(2,1)} custom-call(s32[8]{0:T(128)S(1)} %stack.39.refs_0_, bf16[512,384]{1,0:T(8,128)(2,1)S(1)} %collective-permute-done.5.refs_1_, bf16[512,384]{1,0:T(8,128)(2,1)S(1)} %collective-permute-done.6.refs_2_, bf16[512,384]{1,0:T(8,128)(2,1)S(1)} %collective-permute-done.8.refs_3_, ...), custom_call_target="tpu_custom_call" | custom-call | flops 1600000000 | bytes 4000000 | tf_op jit(solution)/shard_map/pallas_call | solution.py:300
  (45 shorter events, 0.7 us)
Async XLA Ops:
  6.5 17.2 %copy-start.10 = (f32[768]{0:T(1024)S(1)}, f32[768]{0:T(1024)}, u32[]{:S(2)}) copy-start(f32[768]{0:T(1024)} %param.10) | copy-start | bytes 9220
  6.5 73.6 %all-gather.2.cloned.1.call-start = ((), (), s32[]{:S(2)}) async-start(), calls=%async_computation | async-start | bytes 4866048 | tf_op jit(solution)/shard_map/all_gather | solution.py:334
  7.3 25.0 %copy-start.3 = (bf16[512,768]{1,0:T(8,128)(2,1)S(1)}, bf16[512,768]{1,0:T(8,128)(2,1)}, u32[]{:S(2)}) copy-start(bf16[512,768]{1,0:T(8,128)(2,1)} %refs_7_.1) | copy-start | bytes 2359300
  7.3 25.0 %copy-start.4 = (f32[2,32,768]{2,1,0:T(8,128)S(1)}, f32[2,32,768]{2,1,0:T(8,128)}, u32[]{:S(2)}) copy-start(f32[2,32,768]{2,1,0:T(8,128)} %c_ref.3) | copy-start | bytes 589828
  7.3 25.0 %copy-start.6 = (f32[32,768]{1,0:T(8,128)S(1)}, f32[32,768]{1,0:T(8,128)}, u32[]{:S(2)}) copy-start(f32[32,768]{1,0:T(8,128)} %r_ref.5) | copy-start | bytes 294916
  7.3 25.0 %copy-start.7 = (f32[32,768]{1,0:T(8,128)S(1)}, f32[32,768]{1,0:T(8,128)}, u32[]{:S(2)}) copy-start(f32[32,768]{1,0:T(8,128)} %f_ref.5) | copy-start | bytes 294916
  18.1 17.1 %copy-start.8 = (f32[4,2,32,768]{3,2,1,0:T(8,128)S(1)}, f32[4,2,32,768]{3,2,1,0:T(8,128)}, u32[]{:S(2)}) copy-start(f32[4,2,32,768]{3,2,1,0:T(8,128)} %get-tuple-element.18) | copy-start | bytes 2359300
  18.1 1.6 %collective-permute-start = (bf16[2,32,768]{2,1,0:T(8,128)(2,1)}, bf16[2,32,768]{2,1,0:T(8,128)(2,1)S(1)}, u32[]{:S(2)}, u32[]{:S(2)}) collective-permute-start(bf16[2,32,768]{2,1,0:T(8,128)(2,1)} %get-tuple-element.19), channel_id=1, source_target_pairs={{0,4},{4,0},{8,12},{12,8},{16,20},{20,16},{24,28},{28,24},{32,36},... | collective-permute-start | bytes 294920 | tf_op jit(solution)/shard_map/ppermute | solution.py:343
  21.7 15.1 %copy-start.9 = (f32[2,32,768]{2,1,0:T(8,128)S(1)}, f32[2,32,768]{2,1,0:T(8,128)}, u32[]{:S(2)}) copy-start(f32[2,32,768]{2,1,0:T(8,128)} %constant.67.clone.1) | copy-start | bytes 589828
  21.7 5.6 %collective-permute-start.1 = (bf16[2,32,768]{2,1,0:T(8,128)(2,1)S(1)}, bf16[2,32,768]{2,1,0:T(8,128)(2,1)S(1)}, u32[]{:S(2)}, u32[]{:S(2)}) collective-permute-start(bf16[2,32,768]{2,1,0:T(8,128)(2,1)S(1)} %get-tuple-element.31), channel_id=1, source_target_pairs={{0,8},{4,12},{8,0},{12,4},{16,24},{20,28},{24,16},{28,20},{32,40},... | collective-permute-start | bytes 294920 | tf_op jit(solution)/shard_map/ppermute | solution.py:343
  28.4 6.8 %collective-permute-start.2 = (bf16[2,32,768]{2,1,0:T(8,128)(2,1)S(1)}, bf16[2,32,768]{2,1,0:T(8,128)(2,1)S(1)}, u32[]{:S(2)}, u32[]{:S(2)}) collective-permute-start(bf16[2,32,768]{2,1,0:T(8,128)(2,1)S(1)} %get-tuple-element.29), channel_id=1, source_target_pairs={{0,16},{4,20},{8,24},{12,28},{16,0},{20,4},{24,8},{28,12},{32,48},... | collective-permute-start | bytes 294920 | tf_op jit(solution)/shard_map/ppermute | solution.py:343
  35.3 4.7 %collective-permute-start.3 = (bf16[2,32,768]{2,1,0:T(8,128)(2,1)S(1)}, bf16[2,32,768]{2,1,0:T(8,128)(2,1)S(1)}, u32[]{:S(2)}, u32[]{:S(2)}) collective-permute-start(bf16[2,32,768]{2,1,0:T(8,128)(2,1)S(1)} %get-tuple-element.27), channel_id=1, source_target_pairs={{0,32},{4,36},{8,40},{12,44},{16,48},{20,52},{24,56},{28,60},{32,0... | collective-permute-start | bytes 294920 | tf_op jit(solution)/shard_map/ppermute | solution.py:343
  40.1 7.6 %copy-start.2 = (f32[16,2,32,768]{3,2,1,0:T(8,128)S(1)}, f32[16,2,32,768]{3,2,1,0:T(8,128)}, u32[]{:S(2)}) copy-start(f32[16,2,32,768]{3,2,1,0:T(8,128)} %get-tuple-element.16.part_ref) | copy-start | bytes 9437188
  40.1 7.6 %copy-start.5 = (f32[2,32,768]{2,1,0:T(8,128)S(1)}, f32[2,32,768]{2,1,0:T(8,128)}, u32[]{:S(2)}) copy-start(f32[2,32,768]{2,1,0:T(8,128)} %get-tuple-element.17.step_ref) | copy-start | bytes 589828
  40.1 7.6 %collective-permute-start.4 = (bf16[2,32,768]{2,1,0:T(8,128)(2,1)S(1)}, bf16[2,32,768]{2,1,0:T(8,128)(2,1)S(1)}, u32[]{:S(2)}, u32[]{:S(2)}) collective-permute-start(bf16[2,32,768]{2,1,0:T(8,128)(2,1)S(1)} %fusion.4), channel_id=1, source_target_pairs={{0,64},{4,68},{8,72},{12,76},{16,80},{20,84},{24,88},{28,92},{32,9... | collective-permute-start | bytes 294920 | tf_op jit(solution)/shard_map/ppermute | solution.py:343
  52.6 10.3 %collective-permute-start.7 = (bf16[512,384]{1,0:T(8,128)(2,1)S(1)}, bf16[512,384]{1,0:T(8,128)(2,1)S(1)}, u32[]{:S(2)}, u32[]{:S(2)}) collective-permute-start(bf16[512,384]{1,0:T(8,128)(2,1)S(1)} %shard_map.68.refs_1_), channel_id=1, source_target_pairs={{0,1},{1,2},{2,3},{3,0},{4,5},{5,6},{6,7},{7,4},{8,9},{9,10},{10,1... | collective-permute-start | bytes 1179656 | tf_op jit(solution)/shard_map/ppermute | solution.py:361
  58.5 13.3 %collective-permute-start.6 = (bf16[512,384]{1,0:T(8,128)(2,1)S(1)}, bf16[512,384]{1,0:T(8,128)(2,1)S(1)}, u32[]{:S(2)}, u32[]{:S(2)}) collective-permute-start(bf16[512,384]{1,0:T(8,128)(2,1)S(1)} %shard_map.66.refs_2_), channel_id=1, source_target_pairs={{0,3},{1,0},{2,1},{3,2},{4,7},{5,4},{6,5},{7,6},{8,11},{9,8},{10,9... | collective-permute-start | bytes 1179656 | tf_op jit(solution)/shard_map/ppermute | solution.py:362
  59.6 20.5 %collective-permute-start.10 = (bf16[512,384]{1,0:T(8,128)(2,1)S(1)}, bf16[512,384]{1,0:T(8,128)(2,1)S(1)}, u32[]{:S(2)}, u32[]{:S(2)}) collective-permute-start(bf16[512,384]{1,0:T(8,128)(2,1)S(1)} %shard_map.68.refs_1_), channel_id=1, source_target_pairs={{0,3},{1,0},{2,1},{3,2},{4,7},{5,4},{6,5},{7,6},{8,11},{9,8},{10,9... | collective-permute-start | bytes 1179656 | tf_op jit(solution)/shard_map/ppermute | solution.py:362
  60.7 24.6 %collective-permute-start.5 = (bf16[512,384]{1,0:T(8,128)(2,1)S(1)}, bf16[512,384]{1,0:T(8,128)(2,1)S(1)}, u32[]{:S(2)}, u32[]{:S(2)}) collective-permute-start(bf16[512,384]{1,0:T(8,128)(2,1)S(1)} %shard_map.66.refs_2_), channel_id=1, source_target_pairs={{0,1},{1,2},{2,3},{3,0},{4,5},{5,6},{6,7},{7,4},{8,9},{9,10},{10,1... | collective-permute-start | bytes 1179656 | tf_op jit(solution)/shard_map/ppermute | solution.py:361
  62.9 22.4 %collective-permute-start.8 = (bf16[512,384]{1,0:T(8,128)(2,1)S(1)}, bf16[512,384]{1,0:T(8,128)(2,1)S(1)}, u32[]{:S(2)}, u32[]{:S(2)}) collective-permute-start(bf16[512,384]{1,0:T(8,128)(2,1)S(1)} %collective-permute-done.7.refs_3_), channel_id=1, source_target_pairs={{0,1},{1,2},{2,3},{3,0},{4,5},{5,6},{6,7},{7,4},{8,9},{9,10},{10,1... | collective-permute-start | bytes 1179656 | tf_op jit(solution)/shard_map/ppermute | solution.py:363
  71.8 13.5 %collective-permute-start.9 = (bf16[512,384]{1,0:T(8,128)(2,1)S(1)}, bf16[512,384]{1,0:T(8,128)(2,1)}, u32[]{:S(2)}, u32[]{:S(2)}) collective-permute-start(bf16[512,384]{1,0:T(8,128)(2,1)S(1)} %collective-permute-done.6.refs_2_), channel_id=1, source_target_pairs={{0,3},{1,0},{2,1},{3,2},{4,7},{5,4},{6,5},{7,6},{8,11},{9,8},{10,9... | collective-permute-start | bytes 1179656 | tf_op jit(solution)/shard_map/ppermute | solution.py:363
  80.1 2.3 %copy-start = (bf16[3072,768]{1,0:T(8,128)(2,1)S(1)}, bf16[3072,768]{1,0:T(8,128)(2,1)}, u32[]{:S(2)}) copy-start(bf16[3072,768]{1,0:T(8,128)(2,1)} %all-gather.2.cloned.1.call-done.refs_5_) | copy-start | bytes 14155780
  82.5 2.8 %copy-start.1 = (bf16[3072,768]{1,0:T(8,128)(2,1)S(1)}, bf16[3072,768]{1,0:T(8,128)(2,1)}, u32[]{:S(2)}) copy-start(bf16[3072,768]{1,0:T(8,128)(2,1)} %all-gather.2.cloned.1.call-done.refs_5_) | copy-start | bytes 14155780
Sparse Core Ops, SparseCore 0:
  9.6 48.5 all-gather.1

commit v3 on v2

--- a/solution.py
+++ b/solution.py
@@ -163,7 +163,7 @@
                 for k in range(many)
             )
 
-        accs = lax.fori_loop(0, modes, mode, accs, unroll=4)
+        accs = lax.fori_loop(0, modes, mode, accs, unroll=16)
         for k in range(many):
             act_ref[pl.ds((g * many + k) * BLK, BLK), :] = jax.nn.gelu(accs[k]).astype(bf16)
         return 0

time: 96.4 us -> 95.7 us (level)
  transfers between devices with their start and end apart: 12 -> 12, of which waited for: 7 -> 8; matrix products, arithmetic and copies ran while one was open for 4% -> 4% of each run, Pallas kernels for 30% -> 30%
where the time goes in v3:
time: 95.7 us; the launch traced here: 95.4 us
  Pallas kernels  32.3 us (34%)
  waiting for transfers between devices  28.5 us (30%)
  starting transfers between devices  14.8 us (15%)
  between operations  13.7 us (14%)
  other arithmetic  3.63 us (4%)
  local copies, waits for them, and re-layouts  2.55 us (3%)
    ppermute x2, waiting for transfers between devices, local(): down = lax.ppermute(act, 'chan', Y_STEP[3])  15.8 us
    ppermute x5, waiting for transfers between devices, local(): arrived = lax.ppermute(send, 'seq', partners(1 << k))  11.8 us
    pallas_call x1, Pallas kernels, ends(): pl.pallas_call(ends_kernel, grid=(channels // LANES,), in_specs=[pl.Block...  10.8 us
    pallas_call x2, Pallas kernels, finish(): pl.pallas_call(finish_kernel, grid=(count,), in_specs=[pl.BlockSpec((bloc...  9.05 us
    ppermute x5, starting transfers between devices, local(): arrived = lax.ppermute(send, 'seq', partners(1 << k))  8.24 us
    pallas_call x2, Pallas kernels, product(): pl.pallas_call(lambda *refs: product_kernel(len(acts), last, *refs), grid...  6.76 us
    pallas_call x2, Pallas kernels, inner(): pl.pallas_call(inner_kernel, grid=(count,), in_specs=[pl.BlockSpec((token...  5.64 us
    ppermute x2, starting transfers between devices, local(): up = lax.ppermute(act, 'chan', Y_STEP[1])  3.2 us
  transfers between devices with their start and end apart: 12, of which 8 were waited for; matrix products, arithmetic and copies ran while one was open for 4% of the time, Pallas kernels for 30%

profile of v3, /device:TPU:28, one launch (start us, length us, event | category | flops | bytes accessed | tf_op | source)
XLA Modules:
  0.0 95.4 jit_solution(12831142188734321536)
XLA Ops:
  6.5 0.7 all-gather.2.cloned.1.call-update
  7.3 10.8 %shard_map.64 = (f32[16,2,32,768]{3,2,1,0:T(8,128)}, f32[2,32,768]{2,1,0:T(8,128)}, bf16[2,32,768]{2,1,0:T(8,128)(2,1)}, f32[2,32,768]{2,1,0:T(8,128)}, f32[4,2,32,768]{3,2,1,0:T(8,128)}) custom-call(bf16[512,768]{1,0:T(8,128)(2,1)} %refs_7_.1, f32[32,768]{1,0:T(8,128)} %r_ref.5, f32[32,768]{1,0:T(8,128)} %f_ref.5), custom_call_target="tpu_custom_call" | custom-call | flops 1000000000 | bytes 6000000 | tf_op jit(solution)/shard_map/pallas_call | solution.py:183
  18.1 0.1 collective-permute-start
  18.2 1.5 %collective-permute-done = bf16[2,32,768]{2,1,0:T(8,128)(2,1)S(1)} collective-permute-done((bf16[2,32,768]{2,1,0:T(8,128)(2,1)}, bf16[2,32,768]{2,1,0:T(8,128)(2,1)S(1)}, u32[]{:S(2)}, u32[]{:S(2)}) %collective-permute-start) | collective-permute-done | bytes 98336 | tf_op jit(solution)/shard_map/ppermute | solution.py:343
  19.7 0.9 convert_select_fusion.7
  20.7 1.0 %fusion.27 = (f32[1,32,768]{2,1,0:T(8,128)S(1)}, f32[1,32,768]{2,1,0:T(8,128)S(1)}) fusion(f32[2,32,768]{2,1,0:T(8,128)S(1)} %convert_select_fusion.7, f32[4,2,32,768]{3,2,1,0:T(8,128)} %get-tuple-element.18), kind=kLoop, calls=%fused_computation.79 | loop fusion | flops 147456 | bytes 589824 | tf_op jit(solution)/shard_map/sub | solution.py:316
  21.7 2.0 %collective-permute-start.1 = (bf16[2,32,768]{2,1,0:T(8,128)(2,1)S(1)}, bf16[2,32,768]{2,1,0:T(8,128)(2,1)S(1)}, u32[]{:S(2)}, u32[]{:S(2)}) collective-permute-start(bf16[2,32,768]{2,1,0:T(8,128)(2,1)S(1)} %get-tuple-element.31), channel_id=1, source_target_pairs={{0,8},{4,12},{8,0},{12,4},{16,24},{20,28},{24,16},{28,20},{32,40},... | collective-permute-start | bytes 294920 | tf_op jit(solution)/shard_map/ppermute | solution.py:343
  23.7 3.6 %collective-permute-done.1 = bf16[2,32,768]{2,1,0:T(8,128)(2,1)S(1)} collective-permute-done((bf16[2,32,768]{2,1,0:T(8,128)(2,1)S(1)}, bf16[2,32,768]{2,1,0:T(8,128)(2,1)S(1)}, u32[]{:S(2)}, u32[]{:S(2)}) %collective-permute-start.1) | collective-permute-done | bytes 98336 | tf_op jit(solution)/shard_map/ppermute | solution.py:343
  27.4 1.0 %fusion.23 = (f32[1,32,768]{2,1,0:T(8,128)S(1)}, f32[1,32,768]{2,1,0:T(8,128)S(1)}) fusion(f32[2,32,768]{2,1,0:T(8,128)S(1)} %convert_select_fusion.5, f32[4,2,32,768]{3,2,1,0:T(8,128)} %get-tuple-element.18), kind=kLoop, calls=%fused_computation.71 | loop fusion | flops 147456 | bytes 589824 | tf_op jit(solution)/shard_map/sub | solution.py:316
  28.4 3.8 %collective-permute-start.2 = (bf16[2,32,768]{2,1,0:T(8,128)(2,1)S(1)}, bf16[2,32,768]{2,1,0:T(8,128)(2,1)S(1)}, u32[]{:S(2)}, u32[]{:S(2)}) collective-permute-start(bf16[2,32,768]{2,1,0:T(8,128)(2,1)S(1)} %get-tuple-element.29), channel_id=1, source_target_pairs={{0,16},{4,20},{8,24},{12,28},{16,0},{20,4},{24,8},{28,12},{32,48},... | collective-permute-start | bytes 294920 | tf_op jit(solution)/shard_map/ppermute | solution.py:343
  32.3 2.8 %shard_map.67 = (f32[32,2,32,384]{3,2,1,0:T(8,128)S(1)}, f32[512,384]{1,0:T(8,128)S(1)}) custom-call(bf16[512,768]{1,0:T(8,128)(2,1)S(1)} %copy-done.3, f32[32,768]{1,0:T(8,128)S(1)} %copy-done.6, f32[32,768]{1,0:T(8,128)S(1)} %copy-done.7, f32[2,32,768]{2,1,0:T(8,128)S(1)} %copy-done.4, f32[1,768]{1,0:T(1,128)S(1)} %reshape.87.skip_ref), custom_call_target="tpu_custom_call" | custom-call | flops 300000000 | bytes 6000000 | tf_op jit(solution)/shard_map/pallas_call | solution.py:218
  35.3 1.5 %collective-permute-start.3 = (bf16[2,32,768]{2,1,0:T(8,128)(2,1)S(1)}, bf16[2,32,768]{2,1,0:T(8,128)(2,1)S(1)}, u32[]{:S(2)}, u32[]{:S(2)}) collective-permute-start(bf16[2,32,768]{2,1,0:T(8,128)(2,1)S(1)} %get-tuple-element.27), channel_id=1, source_target_pairs={{0,32},{4,36},{8,40},{12,44},{16,48},{20,52},{24,56},{28,60},{32,0... | collective-permute-start | bytes 294920 | tf_op jit(solution)/shard_map/ppermute | solution.py:343
  36.9 2.8 %shard_map.65 = (f32[32,2,32,384]{3,2,1,0:T(8,128)S(1)}, f32[512,384]{1,0:T(8,128)S(1)}) custom-call(bf16[512,768]{1,0:T(8,128)(2,1)S(1)} %copy-done.3, f32[32,768]{1,0:T(8,128)S(1)} %copy-done.6, f32[32,768]{1,0:T(8,128)S(1)} %copy-done.7, f32[2,32,768]{2,1,0:T(8,128)S(1)} %copy-done.4, f32[1,768]{1,0:T(1,128)S(1)} %reshape.87.skip_ref), custom_call_target="tpu_custom_call" | custom-call | flops 300000000 | bytes 6000000 | tf_op jit(solution)/shard_map/pallas_call | solution.py:218
  39.7 0.3 collective-permute-done.3
  40.1 0.8 collective-permute-start.4
  41.2 0.1 fusion.7
  41.3 6.4 %collective-permute-done.4.q_ref = bf16[2,32,768]{2,1,0:T(8,128)(2,1)S(1)} collective-permute-done((bf16[2,32,768]{2,1,0:T(8,128)(2,1)S(1)}, bf16[2,32,768]{2,1,0:T(8,128)(2,1)S(1)}, u32[]{:S(2)}, u32[]{:S(2)}) %collective-permute-start.4) | collective-permute-done | bytes 98336 | tf_op jit(solution)/shard_map/ppermute | solution.py:343
  47.7 4.5 %shard_map.68.refs_1_ = bf16[512,384]{1,0:T(8,128)(2,1)S(1)} custom-call(f32[16,2,32,768]{3,2,1,0:T(8,128)S(1)} %copy-done.2, f32[2,32,768]{2,1,0:T(8,128)S(1)} %copy-done.5, f32[32,2,32,384]{3,2,1,0:T(8,128)S(1)} %get-tuple-element.25.coef_ref, f32[512,384]{1,0:T(8,128)S(1)} %get-tuple-element.26.base_ref, f32[2,32,768]{2,1,0:T(8,128)S(1)} %get-tuple-element.63.own_ref, ...), custom_call_target="tpu_custom_call" | custom-call | flops 500000000 | bytes 6000000 | tf_op jit(solution)/shard_map/pallas_call | solution.py:252
  52.2 1.0 %collective-permute-start.7 = (bf16[512,384]{1,0:T(8,128)(2,1)S(1)}, bf16[512,384]{1,0:T(8,128)(2,1)S(1)}, u32[]{:S(2)}, u32[]{:S(2)}) collective-permute-start(bf16[512,384]{1,0:T(8,128)(2,1)S(1)} %shard_map.68.refs_1_), channel_id=1, source_target_pairs={{0,1},{1,2},{2,3},{3,0},{4,5},{5,6},{6,7},{7,4},{8,9},{9,10},{10,1... | collective-permute-start | bytes 1179656 | tf_op jit(solution)/shard_map/ppermute | solution.py:361
  53.2 4.5 %shard_map.66.refs_2_ = bf16[512,384]{1,0:T(8,128)(2,1)S(1)} custom-call(f32[16,2,32,768]{3,2,1,0:T(8,128)S(1)} %copy-done.2, f32[2,32,768]{2,1,0:T(8,128)S(1)} %copy-done.5, f32[32,2,32,384]{3,2,1,0:T(8,128)S(1)} %get-tuple-element.22.coef_ref, f32[512,384]{1,0:T(8,128)S(1)} %get-tuple-element.23.base_ref, f32[2,32,768]{2,1,0:T(8,128)S(1)} %get-tuple-element.63.own_ref, ...), custom_call_target="tpu_custom_call" | custom-call | flops 500000000 | bytes 6000000 | tf_op jit(solution)/shard_map/pallas_call | solution.py:252
  57.8 1.2 %collective-permute-start.6 = (bf16[512,384]{1,0:T(8,128)(2,1)S(1)}, bf16[512,384]{1,0:T(8,128)(2,1)S(1)}, u32[]{:S(2)}, u32[]{:S(2)}) collective-permute-start(bf16[512,384]{1,0:T(8,128)(2,1)S(1)} %shard_map.66.refs_2_), channel_id=1, source_target_pairs={{0,3},{1,0},{2,1},{3,2},{4,7},{5,4},{6,5},{7,6},{8,11},{9,8},{10,9... | collective-permute-start | bytes 1179656 | tf_op jit(solution)/shard_map/ppermute | solution.py:362
  58.9 1.0 %collective-permute-start.10 = (bf16[512,384]{1,0:T(8,128)(2,1)S(1)}, bf16[512,384]{1,0:T(8,128)(2,1)S(1)}, u32[]{:S(2)}, u32[]{:S(2)}) collective-permute-start(bf16[512,384]{1,0:T(8,128)(2,1)S(1)} %shard_map.68.refs_1_), channel_id=1, source_target_pairs={{0,3},{1,0},{2,1},{3,2},{4,7},{5,4},{6,5},{7,6},{8,11},{9,8},{10,9... | collective-permute-start | bytes 1179656 | tf_op jit(solution)/shard_map/ppermute | solution.py:362
  60.0 2.2 %collective-permute-start.5 = (bf16[512,384]{1,0:T(8,128)(2,1)S(1)}, bf16[512,384]{1,0:T(8,128)(2,1)S(1)}, u32[]{:S(2)}, u32[]{:S(2)}) collective-permute-start(bf16[512,384]{1,0:T(8,128)(2,1)S(1)} %shard_map.66.refs_2_), channel_id=1, source_target_pairs={{0,1},{1,2},{2,3},{3,0},{4,5},{5,6},{6,7},{7,4},{8,9},{9,10},{10,1... | collective-permute-start | bytes 1179656 | tf_op jit(solution)/shard_map/ppermute | solution.py:361
  62.2 0.1 collective-permute-done.7.refs_3_
  62.3 1.1 %collective-permute-start.8 = (bf16[512,384]{1,0:T(8,128)(2,1)S(1)}, bf16[512,384]{1,0:T(8,128)(2,1)S(1)}, u32[]{:S(2)}, u32[]{:S(2)}) collective-permute-start(bf16[512,384]{1,0:T(8,128)(2,1)S(1)} %collective-permute-done.7.refs_3_), channel_id=1, source_target_pairs={{0,1},{1,2},{2,3},{3,0},{4,5},{5,6},{6,7},{7,4},{8,9},{9,10},{10,1... | collective-permute-start | bytes 1179656 | tf_op jit(solution)/shard_map/ppermute | solution.py:363
  63.5 7.7 %collective-permute-done.6.refs_2_ = bf16[512,384]{1,0:T(8,128)(2,1)S(1)} collective-permute-done((bf16[512,384]{1,0:T(8,128)(2,1)S(1)}, bf16[512,384]{1,0:T(8,128)(2,1)S(1)}, u32[]{:S(2)}, u32[]{:S(2)}) %collective-permute-start.6) | collective-permute-done | bytes 393248 | tf_op jit(solution)/shard_map/ppermute | solution.py:362
  71.1 0.1 stack.99.refs_0_
  71.2 0.1 stack.39.refs_0_
  71.3 8.2 %collective-permute-done.10.refs_4_ = bf16[512,384]{1,0:T(8,128)(2,1)S(1)} collective-permute-done((bf16[512,384]{1,0:T(8,128)(2,1)S(1)}, bf16[512,384]{1,0:T(8,128)(2,1)S(1)}, u32[]{:S(2)}, u32[]{:S(2)}) %collective-permute-start.10) | collective-permute-done | bytes 393248 | tf_op jit(solution)/shard_map/ppermute | solution.py:362
  79.4 2.3 %copy-done = bf16[3072,768]{1,0:T(8,128)(2,1)S(1)} copy-done((bf16[3072,768]{1,0:T(8,128)(2,1)S(1)}, bf16[3072,768]{1,0:T(8,128)(2,1)}, u32[]{:S(2)}) %copy-start) | copy-done | bytes 4718616
  81.8 2.8 %shard_map.69.refs_6_ = f32[512,768]{1,0:T(8,128)S(1)} custom-call(s32[8]{0:T(128)S(1)} %stack.99.refs_0_, bf16[512,384]{1,0:T(8,128)(2,1)S(1)} %shard_map.68.refs_1_, bf16[512,384]{1,0:T(8,128)(2,1)S(1)} %shard_map.66.refs_2_, bf16[512,384]{1,0:T(8,128)(2,1)S(1)} %collective-permute-done.7.refs_3_, bf16[512,384]{1,0:T(8,128)(2,1)S(1)} %collective-permute-done.10.refs_4_, ...), custom_call_target="tpu_custom_call" | custom-call | flops 1600000000 | bytes 4000000 | tf_op jit(solution)/shard_map/pallas_call | solution.py:300
  84.6 4.0 %shard_map.70 = bf16[512,768]{1,0:T(8,128)(2,1)} custom-call(s32[8]{0:T(128)S(1)} %stack.39.refs_0_, bf16[512,384]{1,0:T(8,128)(2,1)S(1)} %collective-permute-done.5.refs_1_, bf16[512,384]{1,0:T(8,128)(2,1)S(1)} %collective-permute-done.6.refs_2_, bf16[512,384]{1,0:T(8,128)(2,1)S(1)} %collective-permute-done.8.refs_3_, ...), custom_call_target="tpu_custom_call" | custom-call | flops 1600000000 | bytes 4000000 | tf_op jit(solution)/shard_map/pallas_call | solution.py:300
  (45 shorter events, 0.7 us)
Async XLA Ops:
  6.5 17.2 %copy-start.10 = (f32[768]{0:T(1024)S(1)}, f32[768]{0:T(1024)}, u32[]{:S(2)}) copy-start(f32[768]{0:T(1024)} %param.10) | copy-start | bytes 9220
  6.5 72.9 %all-gather.2.cloned.1.call-start = ((), (), s32[]{:S(2)}) async-start(), calls=%async_computation | async-start | bytes 4866048 | tf_op jit(solution)/shard_map/all_gather | solution.py:334
  7.3 25.0 %copy-start.3 = (bf16[512,768]{1,0:T(8,128)(2,1)S(1)}, bf16[512,768]{1,0:T(8,128)(2,1)}, u32[]{:S(2)}) copy-start(bf16[512,768]{1,0:T(8,128)(2,1)} %refs_7_.1) | copy-start | bytes 2359300
  7.3 25.0 %copy-start.4 = (f32[2,32,768]{2,1,0:T(8,128)S(1)}, f32[2,32,768]{2,1,0:T(8,128)}, u32[]{:S(2)}) copy-start(f32[2,32,768]{2,1,0:T(8,128)} %c_ref.3) | copy-start | bytes 589828
  7.3 25.0 %copy-start.6 = (f32[32,768]{1,0:T(8,128)S(1)}, f32[32,768]{1,0:T(8,128)}, u32[]{:S(2)}) copy-start(f32[32,768]{1,0:T(8,128)} %r_ref.5) | copy-start | bytes 294916
  7.3 25.0 %copy-start.7 = (f32[32,768]{1,0:T(8,128)S(1)}, f32[32,768]{1,0:T(8,128)}, u32[]{:S(2)}) copy-start(f32[32,768]{1,0:T(8,128)} %f_ref.5) | copy-start | bytes 294916
  18.1 17.1 %copy-start.8 = (f32[4,2,32,768]{3,2,1,0:T(8,128)S(1)}, f32[4,2,32,768]{3,2,1,0:T(8,128)}, u32[]{:S(2)}) copy-start(f32[4,2,32,768]{3,2,1,0:T(8,128)} %get-tuple-element.18) | copy-start | bytes 2359300
  18.1 1.6 %collective-permute-start = (bf16[2,32,768]{2,1,0:T(8,128)(2,1)}, bf16[2,32,768]{2,1,0:T(8,128)(2,1)S(1)}, u32[]{:S(2)}, u32[]{:S(2)}) collective-permute-start(bf16[2,32,768]{2,1,0:T(8,128)(2,1)} %get-tuple-element.19), channel_id=1, source_target_pairs={{0,4},{4,0},{8,12},{12,8},{16,20},{20,16},{24,28},{28,24},{32,36},... | collective-permute-start | bytes 294920 | tf_op jit(solution)/shard_map/ppermute | solution.py:343
  21.7 15.1 %copy-start.9 = (f32[2,32,768]{2,1,0:T(8,128)S(1)}, f32[2,32,768]{2,1,0:T(8,128)}, u32[]{:S(2)}) copy-start(f32[2,32,768]{2,1,0:T(8,128)} %constant.67.clone.1) | copy-start | bytes 589828
  21.7 5.6 %collective-permute-start.1 = (bf16[2,32,768]{2,1,0:T(8,128)(2,1)S(1)}, bf16[2,32,768]{2,1,0:T(8,128)(2,1)S(1)}, u32[]{:S(2)}, u32[]{:S(2)}) collective-permute-start(bf16[2,32,768]{2,1,0:T(8,128)(2,1)S(1)} %get-tuple-element.31), channel_id=1, source_target_pairs={{0,8},{4,12},{8,0},{12,4},{16,24},{20,28},{24,16},{28,20},{32,40},... | collective-permute-start | bytes 294920 | tf_op jit(solution)/shard_map/ppermute | solution.py:343
  28.4 6.8 %collective-permute-start.2 = (bf16[2,32,768]{2,1,0:T(8,128)(2,1)S(1)}, bf16[2,32,768]{2,1,0:T(8,128)(2,1)S(1)}, u32[]{:S(2)}, u32[]{:S(2)}) collective-permute-start(bf16[2,32,768]{2,1,0:T(8,128)(2,1)S(1)} %get-tuple-element.29), channel_id=1, source_target_pairs={{0,16},{4,20},{8,24},{12,28},{16,0},{20,4},{24,8},{28,12},{32,48},... | collective-permute-start | bytes 294920 | tf_op jit(solution)/shard_map/ppermute | solution.py:343
  35.3 4.7 %collective-permute-start.3 = (bf16[2,32,768]{2,1,0:T(8,128)(2,1)S(1)}, bf16[2,32,768]{2,1,0:T(8,128)(2,1)S(1)}, u32[]{:S(2)}, u32[]{:S(2)}) collective-permute-start(bf16[2,32,768]{2,1,0:T(8,128)(2,1)S(1)} %get-tuple-element.27), channel_id=1, source_target_pairs={{0,32},{4,36},{8,40},{12,44},{16,48},{20,52},{24,56},{28,60},{32,0... | collective-permute-start | bytes 294920 | tf_op jit(solution)/shard_map/ppermute | solution.py:343
  40.1 7.6 %copy-start.2 = (f32[16,2,32,768]{3,2,1,0:T(8,128)S(1)}, f32[16,2,32,768]{3,2,1,0:T(8,128)}, u32[]{:S(2)}) copy-start(f32[16,2,32,768]{3,2,1,0:T(8,128)} %get-tuple-element.16.part_ref) | copy-start | bytes 9437188
  40.1 7.6 %copy-start.5 = (f32[2,32,768]{2,1,0:T(8,128)S(1)}, f32[2,32,768]{2,1,0:T(8,128)}, u32[]{:S(2)}) copy-start(f32[2,32,768]{2,1,0:T(8,128)} %get-tuple-element.17.step_ref) | copy-start | bytes 589828
  40.1 7.6 %collective-permute-start.4 = (bf16[2,32,768]{2,1,0:T(8,128)(2,1)S(1)}, bf16[2,32,768]{2,1,0:T(8,128)(2,1)S(1)}, u32[]{:S(2)}, u32[]{:S(2)}) collective-permute-start(bf16[2,32,768]{2,1,0:T(8,128)(2,1)S(1)} %fusion.4), channel_id=1, source_target_pairs={{0,64},{4,68},{8,72},{12,76},{16,80},{20,84},{24,88},{28,92},{32,9... | collective-permute-start | bytes 294920 | tf_op jit(solution)/shard_map/ppermute | solution.py:343
  52.2 10.1 %collective-permute-start.7 = (bf16[512,384]{1,0:T(8,128)(2,1)S(1)}, bf16[512,384]{1,0:T(8,128)(2,1)S(1)}, u32[]{:S(2)}, u32[]{:S(2)}) collective-permute-start(bf16[512,384]{1,0:T(8,128)(2,1)S(1)} %shard_map.68.refs_1_), channel_id=1, source_target_pairs={{0,1},{1,2},{2,3},{3,0},{4,5},{5,6},{6,7},{7,4},{8,9},{9,10},{10,1... | collective-permute-start | bytes 1179656 | tf_op jit(solution)/shard_map/ppermute | solution.py:361
  57.8 13.3 %collective-permute-start.6 = (bf16[512,384]{1,0:T(8,128)(2,1)S(1)}, bf16[512,384]{1,0:T(8,128)(2,1)S(1)}, u32[]{:S(2)}, u32[]{:S(2)}) collective-permute-start(bf16[512,384]{1,0:T(8,128)(2,1)S(1)} %shard_map.66.refs_2_), channel_id=1, source_target_pairs={{0,3},{1,0},{2,1},{3,2},{4,7},{5,4},{6,5},{7,6},{8,11},{9,8},{10,9... | collective-permute-start | bytes 1179656 | tf_op jit(solution)/shard_map/ppermute | solution.py:362
  58.9 20.5 %collective-permute-start.10 = (bf16[512,384]{1,0:T(8,128)(2,1)S(1)}, bf16[512,384]{1,0:T(8,128)(2,1)S(1)}, u32[]{:S(2)}, u32[]{:S(2)}) collective-permute-start(bf16[512,384]{1,0:T(8,128)(2,1)S(1)} %shard_map.68.refs_1_), channel_id=1, source_target_pairs={{0,3},{1,0},{2,1},{3,2},{4,7},{5,4},{6,5},{7,6},{8,11},{9,8},{10,9... | collective-permute-start | bytes 1179656 | tf_op jit(solution)/shard_map/ppermute | solution.py:362
  60.0 24.6 %collective-permute-start.5 = (bf16[512,384]{1,0:T(8,128)(2,1)S(1)}, bf16[512,384]{1,0:T(8,128)(2,1)S(1)}, u32[]{:S(2)}, u32[]{:S(2)}) collective-permute-start(bf16[512,384]{1,0:T(8,128)(2,1)S(1)} %shard_map.66.refs_2_), channel_id=1, source_target_pairs={{0,1},{1,2},{2,3},{3,0},{4,5},{5,6},{6,7},{7,4},{8,9},{9,10},{10,1... | collective-permute-start | bytes 1179656 | tf_op jit(solution)/shard_map/ppermute | solution.py:361
  62.3 22.3 %collective-permute-start.8 = (bf16[512,384]{1,0:T(8,128)(2,1)S(1)}, bf16[512,384]{1,0:T(8,128)(2,1)S(1)}, u32[]{:S(2)}, u32[]{:S(2)}) collective-permute-start(bf16[512,384]{1,0:T(8,128)(2,1)S(1)} %collective-permute-done.7.refs_3_), channel_id=1, source_target_pairs={{0,1},{1,2},{2,3},{3,0},{4,5},{5,6},{6,7},{7,4},{8,9},{9,10},{10,1... | collective-permute-start | bytes 1179656 | tf_op jit(solution)/shard_map/ppermute | solution.py:363
  71.1 13.5 %collective-permute-start.9 = (bf16[512,384]{1,0:T(8,128)(2,1)S(1)}, bf16[512,384]{1,0:T(8,128)(2,1)}, u32[]{:S(2)}, u32[]{:S(2)}) collective-permute-start(bf16[512,384]{1,0:T(8,128)(2,1)S(1)} %collective-permute-done.6.refs_2_), channel_id=1, source_target_pairs={{0,3},{1,0},{2,1},{3,2},{4,7},{5,4},{6,5},{7,6},{8,11},{9,8},{10,9... | collective-permute-start | bytes 1179656 | tf_op jit(solution)/shard_map/ppermute | solution.py:363
  79.4 2.3 %copy-start = (bf16[3072,768]{1,0:T(8,128)(2,1)S(1)}, bf16[3072,768]{1,0:T(8,128)(2,1)}, u32[]{:S(2)}) copy-start(bf16[3072,768]{1,0:T(8,128)(2,1)} %all-gather.2.cloned.1.call-done.refs_5_) | copy-start | bytes 14155780
  81.8 2.8 %copy-start.1 = (bf16[3072,768]{1,0:T(8,128)(2,1)S(1)}, bf16[3072,768]{1,0:T(8,128)(2,1)}, u32[]{:S(2)}) copy-start(bf16[3072,768]{1,0:T(8,128)(2,1)} %all-gather.2.cloned.1.call-done.refs_5_) | copy-start | bytes 14155780
Sparse Core Ops, SparseCore 0:
  9.6 48.5 all-gather.1
